TPU v7x, 512 devices: a whole 4x4x16 slice. The times are simulated.
512 devices in a mesh: section: 8 (over y, core), expert: 64 (over x, z).
Axes of the slice: x: 4, y: 4, z: 16, core: 2. Of those that a mesh axis runs over, the one named last changes fastest.
Arguments:
- x_fwd: bfloat16 [8, 6144, 3584], P('section', 'expert'), may hold values from -6 to 6
- ids_fwd: int32 [8, 6144, 8], P('section', 'expert'), may hold values from 0 to 255, as said below
- gates_fwd: float32 [8, 6144, 8], P('section', 'expert'), may hold values from 0.2 to 1
- dy_bwd: bfloat16 [8, 6144, 3584], P('section', 'expert'), may hold values from -6 to 6
- ids_bwd: int32 [8, 6144, 8], P('section', 'expert'), may hold values from 0 to 255, as said below
- gates_bwd: float32 [8, 6144, 8], P('section', 'expert'), may hold values from 0.2 to 1
- saved_hidden: float32 [8, 512, 8192], P('section', None, 'expert'), may hold values from -6 to 6
- w_up: bfloat16 [8, 3584, 8192], P('section', None, 'expert'), may hold values from -0.09375 to 0.09375
- w_down: bfloat16 [8, 8192, 3584], P('section', 'expert'), may hold values from -0.125 to 0.125
Outputs:
- next_fwd: bfloat16 [8, 6144, 3584], P('section', 'expert')
- next_bwd: bfloat16 [8, 6144, 3584], P('section', 'expert')
Inputs may be any that keep to these rules, and one draw needn't show every extreme that they name: `ids_fwd`: each row names 8 different experts, at most one of them below 4. In the rows of one device at most 8 rows name any one expert below 4; in each layer one such expert is named by exactly 8 rows on every device. `ids_bwd`: as for ids_fwd.
All inputs are finite; a program needn't handle non-finite values.
Results may differ from a plain program's by a relative error of at most 0.0021.
Values may be sent and summed in bfloat16 or wider, within the bound.
A program may use at most 128 MiB of HBM per device.

v0:
```python
import jax
import jax.numpy as jnp
from jax import lax
from jax.sharding import PartitionSpec as P

FF = 2048
CAP = 8


def passed_along(shard, axis, by):
    count = lax.axis_size(axis)
    return lax.ppermute(shard, axis, [(i, (i + by) % count) for i in range(count)])


def routing(ids, gates, window):
    expert_iota = jnp.arange(window, dtype=jnp.int32)
    match = ids[:, :, None] == expert_iota[None, None, :]
    routed = jnp.any(match, axis=1).astype(jnp.int32)
    gate_each = jnp.sum(jnp.where(match, gates[:, :, None], jnp.float32(0.0)), axis=1)
    position = jnp.cumsum(routed, axis=0) - routed
    slot_iota = jnp.arange(CAP, dtype=jnp.int32)
    place = (position.T[:, None, :] == slot_iota[None, :, None]) & (routed.T[:, None, :] == 1)
    return (place, gate_each.T)


def pack_rows(place, tokens):
    return jnp.einsum(
        "ect,tf->ecf", place.astype(jnp.bfloat16), tokens, preferred_element_type=jnp.float32
    ).astype(jnp.bfloat16)


def own_group(every, devices, window, group_index):
    shaped = every.reshape(devices, window, every.shape[1], every.shape[2])
    return lax.dynamic_index_in_dim(shaped, group_index, axis=1, keepdims=False)


def combine(tokens, returned, place, gate_each, window, slices):
    width = tokens.shape[1]
    total = jnp.sum(returned.reshape(window, slices, CAP, width).astype(jnp.float32), axis=1)
    weighting = place.astype(jnp.float32) * gate_each[:, None, :]
    branch = jnp.einsum("ect,ecf->tf", weighting, total, precision=lax.Precision.HIGHEST)
    return (tokens.astype(jnp.float32) + branch).astype(jnp.bfloat16)


def per_device(x_fwd, ids_fwd, gates_fwd, dy_bwd, ids_bwd, gates_bwd, saved_hidden, w_up, w_down):
    devices = lax.axis_size("expert")
    slices = FF // w_up.shape[2]
    window = devices // slices
    group_index = lax.axis_index("expert") // slices
    up_weight = w_up[0]
    down_weight = w_down[0]
    tokens = x_fwd[0]
    cotangent = dy_bwd[0]
    saved_rows = saved_hidden[0]
    width = tokens.shape[1]
    place_fwd, gate_fwd = routing(ids_fwd[0], gates_fwd[0], window)
    place_bwd, gate_bwd = routing(ids_bwd[0], gates_bwd[0], window)
    rows_fwd = pack_rows(place_fwd, tokens)
    rows_bwd = pack_rows(place_bwd, cotangent)
    every_fwd = lax.all_gather(rows_fwd, "expert", axis=0, tiled=True)
    received = own_group(every_fwd, devices, window, group_index)
    flat_rows = received.reshape(-1, width)
    hidden = jnp.dot(flat_rows, up_weight, preferred_element_type=jnp.float32)
    activated = jax.nn.silu(hidden).astype(jnp.bfloat16)
    partial_value = jnp.dot(activated, down_weight, preferred_element_type=jnp.float32).astype(
        jnp.bfloat16
    )
    returned_fwd = lax.all_to_all(
        partial_value.reshape(received.shape), "expert", split_axis=0, concat_axis=0, tiled=True
    )
    every_bwd = lax.all_gather(rows_bwd, "expert", axis=0, tiled=True)
    received = own_group(every_bwd, devices, window, group_index)
    flat_rows = received.reshape(-1, width)
    grad_act = jnp.dot(flat_rows, down_weight.T, preferred_element_type=jnp.float32)
    sigmoid_h = jax.nn.sigmoid(saved_rows)
    grad_hidden = (grad_act * sigmoid_h * (1.0 + saved_rows * (1.0 - sigmoid_h))).astype(
        jnp.bfloat16
    )
    partial_value = jnp.dot(grad_hidden, up_weight.T, preferred_element_type=jnp.float32).astype(
        jnp.bfloat16
    )
    returned_bwd = lax.all_to_all(
        partial_value.reshape(received.shape), "expert", split_axis=0, concat_axis=0, tiled=True
    )
    output_fwd = combine(tokens, returned_fwd, place_fwd, gate_fwd, window, slices)
    output_bwd = combine(cotangent, returned_bwd, place_bwd, gate_bwd, window, slices)
    next_fwd = passed_along(output_fwd[None], "section", 1)
    next_bwd = passed_along(output_bwd[None], "section", -1)
    return (next_fwd, next_bwd)


def solution(mesh):
    in_specs = (
        P("section", "expert", None),
        P("section", "expert", None),
        P("section", "expert", None),
        P("section", "expert", None),
        P("section", "expert", None),
        P("section", "expert", None),
        P("section", None, "expert"),
        P("section", None, "expert"),
        P("section", "expert", None),
    )
    out_specs = (P("section", "expert", None), P("section", "expert", None))
    return jax.shard_map(
        per_device, mesh=mesh, in_specs=in_specs, out_specs=out_specs, check_vma=False
    )
```

profile of v0, /device:TPU:1, one launch (start us, length us, event | category | flops | bytes accessed | tf_op | source)
XLA Modules:
  0.0 679.0 jit_solution(18021976724798102817)
XLA Ops:
  7.2 0.0 copy-start
  7.2 0.0 all-gather.5.cloned.1.call-start
  7.2 0.8 fusion.51
  8.0 0.1 copy.41
  8.1 0.1 reduce_window_sum.18
  8.3 0.1 copy.42
  8.3 2.0 convolution_convert_fusion.2
  10.4 0.0 all-gather.5.cloned.1.call-update
  10.4 0.0 all-gather.3.cloned.1.call-start
  10.4 0.7 fusion.53
  11.1 0.1 copy.39
  11.3 0.1 reduce_window_sum.17
  11.4 0.1 copy.40
  11.5 2.0 convolution_convert_fusion.3
  13.5 0.0 all-gather.3.cloned.1.call-update
  13.5 184.5 %all-gather.5.cloned.1.call-done = bf16[256,8,3584]{2,1,0:T(8,128)(2,1)} async-done(((bf16[4,8,3584]{2,1,0:T(8,128)(2,1)}), bf16[256,8,3584]{2,1,0:T(8,128)(2,1)}) %all-gather.5.cloned.1.call-update) | async-done | bytes 14680080 | tf_op jit(solution)/shard_map/all_gather | solution.py:71
  198.0 8.1 %fusion.1 = bf16[64,8,3584]{2,1,0:T(8,128)(2,1)} fusion(bf16[1,3584,128]{2,1,0:T(8,128)(2,1)} %param.16, bf16[64,4,8,3584]{3,2,1,0:T(8,128)(2,1)} %bitcast.109, s32[]{:T(128)S(6)} %select_n.19, bf16[1,128,3584]{2,1,0:T(8,128)(2,1)S(1)} %copy-done, f32[1,512,128]{2,1,0:T(8,128)} %param.15), kind=kOutput, calls=%fused_computation.5 | convolution fusion | flops 941948928 | bytes 9437188 | tf_op jit(solution)/shard_map/dot_general | solution.py:79
  206.1 10.8 %all-to-all-start.1 = ((bf16[64,8,3584]{2,1,0:T(8,128)(2,1)}), bf16[64,8,3584]{2,1,0:T(8,128)(2,1)}, u32[]{:S(2)}, u32[]{:S(2)}) async-start(bf16[64,8,3584]{2,1,0:T(8,128)(2,1)} %fusion.1), calls=%async_computation.1 | async-start | bytes 7340032 | tf_op jit(solution)/shard_map/all_to_all | solution.py:82
  216.9 253.8 %all-gather.3.cloned.1.call-done = bf16[256,8,3584]{2,1,0:T(8,128)(2,1)} async-done(((bf16[4,8,3584]{2,1,0:T(8,128)(2,1)}), bf16[256,8,3584]{2,1,0:T(8,128)(2,1)}) %all-gather.3.cloned.1.call-update) | async-done | bytes 14680080 | tf_op jit(solution)/shard_map/all_gather | solution.py:60
  470.7 7.8 %fusion = bf16[64,8,3584]{2,1,0:T(8,128)(2,1)} fusion(bf16[1,128,3584]{2,1,0:T(8,128)(2,1)S(1)} %copy-done, bf16[1,3584,128]{2,1,0:T(8,128)(2,1)S(1)} %copy-done.1, bf16[64,4,8,3584]{3,2,1,0:T(8,128)(2,1)} %bitcast.110, s32[]{:T(128)S(6)} %select_n.19), kind=kOutput, calls=%fused_computation.4 | convolution fusion | flops 941686784 | bytes 9175044 | tf_op jit(solution)/shard_map/dot_general | solution.py:65
  478.6 12.3 %all-to-all-start = ((bf16[64,8,3584]{2,1,0:T(8,128)(2,1)}), bf16[64,8,3584]{2,1,0:T(8,128)(2,1)}, u32[]{:S(2)}, u32[]{:S(2)}) async-start(bf16[64,8,3584]{2,1,0:T(8,128)(2,1)} %fusion), calls=%async_computation | async-start | bytes 7340032 | tf_op jit(solution)/shard_map/all_to_all | solution.py:68
  490.9 0.0 copy-start.2
  491.0 2.6 convert_reduce_fusion
  493.7 1.3 fusion.7
  495.0 0.8 collective-permute-start.1
  495.8 154.8 %all-to-all-done = bf16[64,8,3584]{2,1,0:T(8,128)(2,1)} async-done(((bf16[64,8,3584]{2,1,0:T(8,128)(2,1)}), bf16[64,8,3584]{2,1,0:T(8,128)(2,1)}, u32[]{:S(2)}, u32[]{:S(2)}) %all-to-all-start) | async-done | bytes 3670048 | tf_op jit(solution)/shard_map/all_to_all | solution.py:68
  650.6 2.6 convert_reduce_fusion.1
  653.2 1.3 fusion.6
  654.5 8.0 %collective-permute-start = (bf16[1,96,3584]{2,1,0:T(8,128)(2,1)S(1)}, bf16[1,96,3584]{2,1,0:T(8,128)(2,1)S(1)}, u32[]{:S(2)}, u32[]{:S(2)}) collective-permute-start(bf16[1,96,3584]{2,1,0:T(8,128)(2,1)S(1)} %fusion.6), channel_id=1, source_target_pairs={{0,64},{64,128},{128,192},{192,256},{256,320},{320,384},{384,448},... | collective-permute-start | bytes 2064392 | tf_op jit(solution)/shard_map/ppermute | solution.py:12
  662.5 7.9 %collective-permute-done = bf16[1,96,3584]{2,1,0:T(8,128)(2,1)S(1)} collective-permute-done((bf16[1,96,3584]{2,1,0:T(8,128)(2,1)S(1)}, bf16[1,96,3584]{2,1,0:T(8,128)(2,1)S(1)}, u32[]{:S(2)}, u32[]{:S(2)}) %collective-permute-start) | collective-permute-done | bytes 688160 | tf_op jit(solution)/shard_map/ppermute | solution.py:12
  670.4 0.8 copy.45
  671.3 0.8 copy.46
  (22 shorter events, 0.1 us)
Async XLA Ops:
  7.2 190.9 %copy-start = (bf16[1,128,3584]{2,1,0:T(8,128)(2,1)S(1)}, bf16[1,128,3584]{2,1,0:T(8,128)(2,1)}, u32[]{:S(2)}) copy-start(bf16[1,128,3584]{2,1,0:T(8,128)(2,1)} %param.17) | copy-start | bytes 2752516
  7.2 190.8 %all-gather.5.cloned.1.call-start = ((), (), s32[]{:S(2)}) async-start(), calls=%async_computation.3 | async-start | bytes 14909440 | tf_op jit(solution)/shard_map/all_gather | solution.py:71
  10.4 460.4 %all-gather.3.cloned.1.call-start = ((), (), s32[]{:S(2)}) async-start(), calls=%async_computation.2 | async-start | bytes 14909440 | tf_op jit(solution)/shard_map/all_gather | solution.py:60
  206.1 264.6 %copy-start.1 = (bf16[1,3584,128]{2,1,0:T(8,128)(2,1)S(1)}, bf16[1,3584,128]{2,1,0:T(8,128)(2,1)}, u32[]{:S(2)}) copy-start(bf16[1,3584,128]{2,1,0:T(8,128)(2,1)} %param.16) | copy-start | bytes 2752516
  206.1 272.4 %all-to-all-start.1 = ((bf16[64,8,3584]{2,1,0:T(8,128)(2,1)}), bf16[64,8,3584]{2,1,0:T(8,128)(2,1)}, u32[]{:S(2)}, u32[]{:S(2)}) async-start(bf16[64,8,3584]{2,1,0:T(8,128)(2,1)} %fusion.1), calls=%async_computation.1 | async-start | bytes 7340032 | tf_op jit(solution)/shard_map/all_to_all | solution.py:82
  478.6 12.4 %copy-start.4 = (s32[1,96,8]{1,2,0:T(8,128)S(1)}, s32[1,96,8]{1,2,0:T(8,128)}, u32[]{:S(2)}) copy-start(s32[1,96,8]{1,2,0:T(8,128)} %param.13) | copy-start | bytes 9220
  478.6 12.4 %copy-start.6 = (f32[1,96,8]{1,2,0:T(8,128)S(1)}, f32[1,96,8]{1,2,0:T(8,128)}, u32[]{:S(2)}) copy-start(f32[1,96,8]{1,2,0:T(8,128)} %param.14) | copy-start | bytes 9220
  478.6 12.4 %copy-start.5 = (s32[1,96,8]{1,2,0:T(8,128)S(1)}, s32[1,96,8]{1,2,0:T(8,128)}, u32[]{:S(2)}) copy-start(s32[1,96,8]{1,2,0:T(8,128)} %param.10) | copy-start | bytes 9220
  478.6 12.4 %copy-start.7 = (f32[1,96,8]{1,2,0:T(8,128)S(1)}, f32[1,96,8]{1,2,0:T(8,128)}, u32[]{:S(2)}) copy-start(f32[1,96,8]{1,2,0:T(8,128)} %param.11) | copy-start | bytes 9220
  478.6 172.0 %all-to-all-start = ((bf16[64,8,3584]{2,1,0:T(8,128)(2,1)}), bf16[64,8,3584]{2,1,0:T(8,128)(2,1)}, u32[]{:S(2)}, u32[]{:S(2)}) async-start(bf16[64,8,3584]{2,1,0:T(8,128)(2,1)} %fusion), calls=%async_computation | async-start | bytes 7340032 | tf_op jit(solution)/shard_map/all_to_all | solution.py:68
  490.9 2.8 copy-start.2
  493.7 159.5 %copy-start.3 = (bf16[1,96,3584]{2,1,0:T(8,128)(2,1)S(1)}, bf16[1,96,3584]{2,1,0:T(8,128)(2,1)}, u32[]{:S(2)}) copy-start(bf16[1,96,3584]{2,1,0:T(8,128)(2,1)} %param.9) | copy-start | bytes 2064388
  495.0 167.5 %collective-permute-start.1 = (bf16[1,96,3584]{2,1,0:T(8,128)(2,1)S(1)}, bf16[1,96,3584]{2,1,0:T(8,128)(2,1)S(1)}, u32[]{:S(2)}, u32[]{:S(2)}) collective-permute-start(bf16[1,96,3584]{2,1,0:T(8,128)(2,1)S(1)} %fusion.7), channel_id=1, source_target_pairs={{0,448},{64,0},{128,64},{192,128},{256,192},{320,256},{384,320},{4... | collective-permute-start | bytes 2064392 | tf_op jit(solution)/shard_map/ppermute | solution.py:12
  654.5 15.9 %collective-permute-start = (bf16[1,96,3584]{2,1,0:T(8,128)(2,1)S(1)}, bf16[1,96,3584]{2,1,0:T(8,128)(2,1)S(1)}, u32[]{:S(2)}, u32[]{:S(2)}) collective-permute-start(bf16[1,96,3584]{2,1,0:T(8,128)(2,1)S(1)} %fusion.6), channel_id=1, source_target_pairs={{0,64},{64,128},{128,192},{192,256},{256,320},{320,384},{384,448},... | collective-permute-start | bytes 2064392 | tf_op jit(solution)/shard_map/ppermute | solution.py:12
Sparse Core Ops, SparseCore 0:
  11.5 186.4 all-gather.4
  201.5 269.1 all-gather.2
where the time goes:
time: 680 us; the launch traced here: 679 us
  waiting for transfers between devices  601 us (88%)
  starting transfers between devices  32 us (5%)
  matrix products  22.6 us (3%)
  between operations  14.2 us (2%)
  other arithmetic  7.06 us (1%)
    all_gather x1, waiting for transfers between devices, per_device(): every_fwd = lax.all_gather(rows_fwd, 'expert', axis=0, tiled=True)  254 us
    all_gather x1, waiting for transfers between devices, per_device(): every_bwd = lax.all_gather(rows_bwd, 'expert', axis=0, tiled=True)  184 us
    all_to_all x2, waiting for transfers between devices, per_device(): lax.all_to_all(partial_value.reshape(received.shape), 'expert', split_axi...  155 us
    all_to_all x2, starting transfers between devices, per_device(): lax.all_to_all(partial_value.reshape(received.shape), 'expert', split_axi...  23.1 us
  transfers between devices with their start and end apart: 6, of which 4 were waited for; matrix products, arithmetic and copies ran while one was open for 4% of the time, Pallas kernels for 0%

commit v1 on v0

v1 whole, which is shorter than its diff:
```python
import functools

import jax
import jax.numpy as jnp
from jax import lax
from jax.experimental import pallas as pl
from jax.experimental.pallas import tpu as pltpu
from jax.sharding import PartitionSpec as P

MESH = pl.DeviceIdType.MESH
CAP = 8
SUB = 2 * CAP
FF = 2048
f32 = jnp.float32
bf16 = jnp.bfloat16


def tile_of(width):
    return 512 if width % 512 == 0 else 128


def routing(ids, gates, window):
    rows, choices = ids.shape
    span = SUB * window
    lane = lax.broadcasted_iota(jnp.int32, (rows, 2 * span), 1)
    expert = lax.div(lax.rem(lane, span), SUB)
    slot = lax.rem(lane, CAP)
    same_half = lax.div(lane, span) == lax.div(lax.rem(lane, SUB), CAP)
    routed = jnp.zeros((rows, 2 * span), f32)
    gate = jnp.zeros((rows, 2 * span), f32)
    for k in range(choices):
        match = ids[:, k : k + 1] == expert
        routed = jnp.where(match, 1.0, routed)
        gate = gate + jnp.where(match, gates[:, k : k + 1], 0.0)
    earlier = lax.broadcasted_iota(jnp.int32, (rows, rows), 1) < lax.broadcasted_iota(
        jnp.int32, (rows, rows), 0
    )
    position = jnp.dot(
        jnp.where(earlier, 1.0, 0.0).astype(bf16), routed.astype(bf16), preferred_element_type=f32
    )
    taken = (routed > 0.5) & (position == slot.astype(f32)) & same_half
    place = jnp.where(taken, 1.0, 0.0)
    return place, place * gate


def kernel(
    nsec, nx, nz,
    x_hbm, dy_hbm, idf_ref, gf_ref, idb_ref, gb_ref, saved_hbm, up_hbm, down_hbm,
    outf_hbm, outb_hbm,
    xin, rows, gall, gown, upw, downw, saved, ag, rs, stage, part, plr, near, near_plr, ysend, yrecv, obuf,
    load_sem, out_sem, xs_send, xs_recv, gs_send, gs_recv, ag_send, ag_recv, rs_send, rs_recv,
    near_send, near_recv, y_send, y_recv,
):
    half = nz // 2
    tokens, width = xin.shape[1], xin.shape[2]
    span = SUB * nx
    fold = width // 2
    hid = upw.shape[1] // 2
    tile = tile_of(width)
    ftile = tile_of(fold)
    early = range(nx // 2)
    late = range(nx // 2, nx)

    sec = lax.axis_index("section")
    me = lax.axis_index("expert")
    mx, mz = lax.div(me, nz), lax.rem(me, nz)
    right = (sec, mx * nz + lax.rem(mz + 1, nz))
    left = (sec, mx * nz + lax.rem(mz + nz - 1, nz))
    sec_up, sec_down = lax.rem(sec + 1, nsec), lax.rem(sec + nsec - 1, nsec)
    columns = [lax.rem(mx + i, nx) for i in range(nx)]
    targets = [lax.rem(mx + nx - i, nx) for i in range(nx)]
    out_way = (right, left)
    back_way = (left, right)

    def remote(src, dst, send, recv, device):
        return pltpu.make_async_remote_copy(
            src_ref=src, dst_ref=dst, send_sem=send, recv_sem=recv, device_id=device, device_id_type=MESH
        )

    def sub(i):
        return pl.ds(i * SUB, SUB)

    def sub_at(index):
        return pl.ds(pl.multiple_of(index * SUB, SUB), SUB)

    loads = [
        pltpu.make_async_copy(x_hbm, xin.at[0], load_sem.at[0]),
        pltpu.make_async_copy(dy_hbm, xin.at[1], load_sem.at[1]),
        pltpu.make_async_copy(up_hbm, upw.at[:, pl.ds(0, hid)], load_sem.at[2]),
        pltpu.make_async_copy(down_hbm, downw.at[pl.ds(0, hid)], load_sem.at[3]),
        pltpu.make_async_copy(saved_hbm, saved, load_sem.at[4]),
    ]
    for load in loads:
        load.start()

    peers = [right, left]
    peers += [(sec, columns[i] * nz + mz) for i in range(1, nx)]
    peers += [(s, columns[i] * nz + mz) for s in (sec_up, sec_down) for i in range(nx)]
    barrier = pltpu.get_barrier_semaphore()
    for peer in peers:
        pl.semaphore_signal(barrier, inc=1, device_id=peer, device_id_type=MESH)

    place_f, weight_f = routing(idf_ref[...], gf_ref[...], nx)
    place_b, weight_b = routing(idb_ref[...], gb_ref[...], nx)
    plr[0] = place_f.astype(bf16)
    plr[1] = place_b.astype(bf16)
    first = lax.broadcasted_iota(jnp.int32, place_f.shape, 1) < span
    chosen = jnp.where(first, place_f, place_b).T.astype(bf16)
    weight = jnp.sum(jnp.where(first, weight_f, weight_b).T, axis=1, keepdims=True)
    gall[...] = jnp.broadcast_to(weight[:span] + weight[span:], gall.shape)
    chosen_f, chosen_b = chosen[:span], chosen[span:]
    loads[0].wait()
    loads[1].wait()

    @pl.loop(0, width // tile)
    def _(step):
        cols = pl.ds(pl.multiple_of(step * tile, tile), tile)
        rows[:, cols] = (
            jnp.dot(chosen_f, xin[0, :, cols], preferred_element_type=f32)
            + jnp.dot(chosen_b, xin[1, :, cols], preferred_element_type=f32)
        ).astype(bf16)

    ag[0, 0, sub(0)] = rows[sub_at(mx)]
    gown[sub(0)] = gall[sub_at(mx)]
    pl.semaphore_wait(barrier, len(peers))

    def row_copy(i):
        device = (sec, targets[i] * nz + mz)
        return remote(
            rows.at[sub_at(targets[i])], ag.at[0, 0, sub(i)], xs_send.at[i - 1], xs_recv.at[i - 1], device
        )

    def gate_copy(i):
        device = (sec, targets[i] * nz + mz)
        return remote(
            gall.at[sub_at(targets[i])], gown.at[sub(i)], gs_send.at[i - 1], gs_recv.at[i - 1], device
        )

    def out_copy(s, d, i, own=False):
        src = ag.at[0, 0, sub(i)] if own else ag.at[s, d, sub(i)]
        send = ag_send.at[d] if own else ag_send.at[s + 1]
        return remote(src, ag.at[s + 1, d, sub(i)], send, ag_recv.at[s + 1, d, i], out_way[d])

    def far_copy(d, i):
        send = ag_send.at[half if d == 0 else half + 1]
        return remote(ag.at[half - 1, d, sub(i)], ag.at[0, 1, sub(i)], send, ag_recv.at[0, 1, i], out_way[d])

    for i in range(1, nx):
        row_copy(i).start()
    for d in range(2):
        out_copy(0, d, 0, own=True).start()
    for i in range(1, nx):
        gate_copy(i).start()

    next_of = ((sec_up, me), (sec_down, me))
    near_copies = [
        remote(src.at[h], dst.at[h], near_send.at[h, k], near_recv.at[h, k], next_of[h])
        for h in range(2)
        for k, (src, dst) in enumerate(((xin, near), (plr, near_plr)))
    ]
    for copy in near_copies:
        copy.start()

    for i in range(1, nx):
        row_copy(i).wait_recv()
        for d in range(2):
            out_copy(0, d, i, own=True).start()

    loads[2].wait()
    loads[3].wait()
    loads[4].wait()

    @pl.loop(0, width // tile)
    def _(step):
        cols = pl.ds(pl.multiple_of(step * tile, tile), tile)
        upw[cols, pl.ds(hid, hid)] = downw[pl.ds(0, hid), cols].T
        downw[pl.ds(hid, hid), cols] = upw[cols, pl.ds(0, hid)].T

    @pl.loop(0, nx)
    def _(column):
        value = saved[column]
        sig = jax.nn.sigmoid(value)
        saved[column] = sig * (1.0 + value * (1.0 - sig))

    def compute(s, sources):
        def add_up(step, total):
            cols = pl.ds(pl.multiple_of(step * tile, tile), tile)
            block = ag[s, :, :, cols].reshape(2 * span, tile)
            return total + jnp.dot(block, upw[cols, :], preferred_element_type=f32)

        total = lax.fori_loop(0, width // tile, add_up, jnp.zeros((2 * span, 2 * hid), f32))
        total = total.reshape(2 * nx, 2, CAP, 2 * hid)
        forward = total[:, 0, :, :hid]
        forward = forward * jax.nn.sigmoid(forward)
        slope = jnp.stack([saved[columns[i], source] for source in sources for i in range(nx)])
        backward = total[:, 1, :, hid:] * slope
        none = jnp.zeros_like(forward)
        inner = jnp.stack(
            [jnp.concatenate([forward, none], axis=-1), jnp.concatenate([none, backward], axis=-1)], axis=1
        )
        inner = inner.reshape(2 * span, 2 * hid).astype(bf16)

        @pl.loop(0, width // tile)
        def _(step):
            cols = pl.ds(pl.multiple_of(step * tile, tile), tile)
            result = jnp.dot(inner, downw[:, cols], preferred_element_type=f32)
            part[s, :, :, cols] = result.reshape(2, span, tile)

    def both(s):
        return (lax.rem(mz + nz - s, nz), lax.rem(mz + s, nz))

    @pl.loop(1, half - 1)
    def _(s):
        for i in range(nx):
            for d in range(2):
                out_copy(s - 1, d, i).wait_recv()
                out_copy(s, d, i).start()
        compute(s, both(s))

    for i in range(nx):
        for d in range(2):
            out_copy(half - 2, d, i).wait_recv()
            if i in (early, late)[d]:
                far_copy(d, i).start()
    compute(half - 1, both(half - 1))

    def back_copy(s, d, i):
        return remote(
            rs.at[s, d, sub(i)], rs.at[s - 1, d, sub(i)], rs_send.at[s], rs_recv.at[s - 1, d, i], back_way[d]
        )

    def first_copy(d, i):
        return remote(stage.at[sub(i)], rs.at[half - 1, d, sub(i)], rs_send.at[0], rs_recv.at[half - 1, d, i], back_way[d])

    for d in range(2):
        for i in (late, early)[d]:
            rs[half - 1, d, sub(i)] = part[half - 1, d, sub(i)].astype(bf16)
            back_copy(half - 1, d, i).start()
    for i in range(nx):
        far_copy(0 if i in early else 1, i).wait_recv()
    compute(0, (mz, lax.rem(mz + half, nz)))
    for i in range(nx):
        stage[sub(i)] = part[0, 1, sub(i)].astype(bf16)
        first_copy(0 if i in early else 1, i).start()

    def pass_on(s, d, i):
        rs[s, d, sub(i)] = (rs[s, d, sub(i)].astype(f32) + part[s, d, sub(i)]).astype(bf16)
        back_copy(s, d, i).start()

    for k in range(nx // 2):
        for d in range(2):
            i = (early, late)[d][k]
            first_copy(d, i).wait_recv()
            pass_on(half - 1, d, i)

    order = (list(late) + list(early), list(early) + list(late))

    @pl.loop(1, half - 1)
    def _(step):
        s = half - 1 - step
        for k in range(nx):
            for d in range(2):
                back_copy(s + 1, d, order[d][k]).wait_recv()
                pass_on(s, d, order[d][k])
        remote(ag.at[s], ag.at[s], ag_send.at[s + 1], ag_recv.at[s, 0, 0], right).wait_send()

    for i in range(1, nx):
        gate_copy(i).wait_recv()

    def y_copy(h, i):
        device = ((sec_up, sec_down)[h], columns[i] * nz + mz)
        return remote(ysend.at[h, sub(i)], yrecv.at[h, sub_at(mx)], y_send.at[h], y_recv.at[h, mx], device)

    for k in range(nx):
        i = (list(early) + list(late))[(k % 2) * (nx // 2) + k // 2]
        for d in range(2):
            back_copy(1, d, i).wait_recv()
        gate = gown[sub(i), 0:1]

        @pl.loop(0, fold // ftile)
        def _(step):
            halves = []
            for side in range(2):
                cols = pl.ds(pl.multiple_of(side * fold + step * ftile, 128), ftile)
                total = part[0, 0, sub(i), cols]
                for d in range(2):
                    total = total + rs[0, d, sub(i), cols].astype(f32)
                halves.append(ag[0, 0, sub(i), cols].astype(f32) + gate * total)
            cols = pl.ds(pl.multiple_of(step * ftile, 128), ftile)
            for h in range(2):
                picked = [value[h * CAP : (h + 1) * CAP] for value in halves]
                ysend[h, sub(i), cols] = jnp.concatenate(picked, axis=0).astype(bf16)

        for h in range(2):
            y_copy(h, i).start()

    for copy in near_copies:
        copy.wait()
    for h in range(2):
        for e in range(nx):
            remote(ysend.at[h, sub(e)], yrecv.at[h, sub(e)], y_send.at[h], y_recv.at[h, e], next_of[h]).wait_recv()
        place = near_plr[h]
        with_share = jnp.max(place.astype(f32), axis=1, keepdims=True) > 0.5
        for side in range(2):
            spots = place[:, side * span : (side + 1) * span]

            @pl.loop(0, fold // ftile)
            def _(step):
                part_cols = pl.ds(pl.multiple_of(step * ftile, 128), ftile)
                cols = pl.ds(pl.multiple_of(side * fold + step * ftile, 128), ftile)
                moved = jnp.dot(spots, yrecv[h, :, part_cols], preferred_element_type=f32)
                kept = near[h, :, cols].astype(f32)
                obuf[h, :, cols] = jnp.where(with_share, moved, kept).astype(bf16)

        pltpu.make_async_copy(obuf.at[h], (outf_hbm, outb_hbm)[h], out_sem.at[h]).start()

    for i in range(1, nx):
        row_copy(i).wait_send()
        gate_copy(i).wait_send()
    for d in range(2):
        remote(ag.at[0, 0], ag.at[1, d], ag_send.at[d], ag_recv.at[1, d, 0], right).wait_send()
        far_rows = pl.ds((early, late)[d][0] * SUB, SUB * (nx // 2))
        far = ag.at[half - 1, d, far_rows]
        remote(far, far, ag_send.at[half + d], ag_recv.at[0, 1, 0], right).wait_send()
        remote(ysend.at[d], yrecv.at[d], y_send.at[d], y_recv.at[d, 0], right).wait_send()
    remote(stage, rs.at[0, 0], rs_send.at[0], rs_recv.at[0, 0, 0], right).wait_send()
    for s in range(1, half):
        remote(rs.at[s], rs.at[s - 1], rs_send.at[s], rs_recv.at[0, 0, 0], right).wait_send()
    for h in range(2):
        pltpu.make_async_copy(obuf.at[h], (outf_hbm, outb_hbm)[h], out_sem.at[h]).wait()


def per_device(x_fwd, ids_fwd, gates_fwd, dy_bwd, ids_bwd, gates_bwd, saved_hidden, w_up, w_down):
    nsec = lax.axis_size("section")
    devices = lax.axis_size("expert")
    hid = w_up.shape[2]
    nz = FF // hid
    nx = devices // nz
    half = nz // 2
    tokens, width = x_fwd.shape[1:]
    span = SUB * nx
    any_space = pl.BlockSpec(memory_space=pl.ANY)
    vmem = pl.BlockSpec(memory_space=pltpu.VMEM)
    dma = pltpu.SemaphoreType.DMA
    outs = pl.pallas_call(
        functools.partial(kernel, nsec, nx, nz),
        out_shape=[jax.ShapeDtypeStruct((tokens, width), bf16)] * 2,
        in_specs=[any_space, any_space, vmem, vmem, vmem, vmem, any_space, any_space, any_space],
        out_specs=[any_space, any_space],
        scratch_shapes=[
            pltpu.VMEM((2, tokens, width), bf16),
            pltpu.VMEM((span, width), bf16),
            pltpu.VMEM((span, 128), f32),
            pltpu.VMEM((span, 128), f32),
            pltpu.VMEM((width, 2 * hid), bf16),
            pltpu.VMEM((2 * hid, width), bf16),
            pltpu.VMEM((nx, nz, CAP, hid), f32),
            pltpu.VMEM((half, 2, span, width), bf16),
            pltpu.VMEM((half, 2, span, width), bf16),
            pltpu.VMEM((span, width), bf16),
            pltpu.VMEM((half, 2, span, width), f32),
            pltpu.VMEM((2, tokens, 2 * span), bf16),
            pltpu.VMEM((2, tokens, width), bf16),
            pltpu.VMEM((2, tokens, 2 * span), bf16),
            pltpu.VMEM((2, span, width // 2), bf16),
            pltpu.VMEM((2, span, width // 2), bf16),
            pltpu.VMEM((2, tokens, width), bf16),
            dma((5,)), dma((2,)),
            dma((nx - 1,)), dma((nx - 1,)), dma((nx - 1,)), dma((nx - 1,)),
            dma((half + 2,)), dma((half, 2, nx)),
            dma((half,)), dma((half, 2, nx)),
            dma((2, 2)), dma((2, 2)), dma((2,)), dma((2, nx)),
        ],
        compiler_params=pltpu.CompilerParams(
            collective_id=0, has_side_effects=True, vmem_limit_bytes=56 * 1024 * 1024
        ),
    )(
        x_fwd[0], dy_bwd[0], ids_fwd[0], gates_fwd[0], ids_bwd[0], gates_bwd[0],
        saved_hidden[0].reshape(nx, nz, CAP, hid), w_up[0], w_down[0],
    )
    return (outs[0][None], outs[1][None])


def solution(mesh):
    in_specs = (
        P("section", "expert", None),
        P("section", "expert", None),
        P("section", "expert", None),
        P("section", "expert", None),
        P("section", "expert", None),
        P("section", "expert", None),
        P("section", None, "expert"),
        P("section", None, "expert"),
        P("section", "expert", None),
    )
    out_specs = (P("section", "expert", None), P("section", "expert", None))
    return jax.shard_map(
        per_device, mesh=mesh, in_specs=in_specs, out_specs=out_specs, check_vma=False
    )
```

time: 680 us -> 190 us (0.28)
  waiting for transfers between devices: 601 us -> 0 us
  Pallas kernels: 0 us -> 183 us
  starting transfers between devices: 32 us -> 0 us
  matrix products: 22.6 us -> 0 us
  between operations: 14.2 us -> 0.66 us
  other arithmetic: 7.06 us -> 0 us
    all_gather x2 -> x0, waiting for transfers between devices: 438 us -> none  [the longest x1 254 us: per_device(): every_fwd = lax.all_gather(rows_fwd, 'expert', axis=0, tiled=True)]
    pallas_call x0 -> x1, Pallas kernels: none -> 183 us  [per_device(): pl.pallas_call(functools.partial(kernel, nsec, nx, nz), out_shape=[jax.Sh...]
    all_to_all x2 -> x0, waiting for transfers between devices: 155 us -> none  [per_device(): lax.all_to_all(partial_value.reshape(received.shape), 'expert', split_axi...]
    all_to_all x2 -> x0, starting transfers between devices: 23.1 us -> none  [per_device(): lax.all_to_all(partial_value.reshape(received.shape), 'expert', split_axi...]
    dot_general x6 -> x0, matrix products: 22.6 us -> none  [the longest x1 8.11 us: per_device(): jnp.dot(grad_hidden, up_weight.T, preferred_element_type=jnp.float32)]
    ppermute x2 -> x0, starting transfers between devices: 8.8 us -> none  [passed_along(): lax.ppermute(shard, axis, [(i, (i + by) % count) for i in range(count)])]
    ppermute x2 -> x0, waiting for transfers between devices: 7.88 us -> none  [passed_along(): lax.ppermute(shard, axis, [(i, (i + by) % count) for i in range(count)])]
  transfers between devices with their start and end apart: 6 -> 0, of which waited for: 4 -> 0; matrix products, arithmetic and copies ran while one was open for 4% -> 0% of each run, Pallas kernels for 0% -> 0%
where the time goes in v1:
time: 190 us
  Pallas kernels  183 us (96%)
  local copies, waits for them, and re-layouts  6.43 us (3%)
    pallas_call x1, Pallas kernels, per_device(): pl.pallas_call(functools.partial(kernel, nsec, nx, nz), out_shape=[jax.Sh...  183 us
    unnamed x16, local copies, waits for them, and re-layouts  6.43 us

profile of v1, /device:TPU:1, one launch (start us, length us, event | category | flops | bytes accessed | tf_op | source)
XLA Modules:
  0.0 190.1 jit_solution(8023609446721979150)
XLA Ops:
  0.6 0.0 copy-start.1
  0.6 0.7 copy-done.1
  1.3 0.0 copy-start.2
  1.3 0.7 copy.11
  2.0 0.0 copy-done.2
  2.0 0.0 copy-start.3
  2.0 0.7 copy.12
  2.7 0.0 copy-done.3
  2.8 0.0 copy-start.4
  2.8 0.7 copy.13
  3.5 0.0 copy-done.4
  3.5 0.7 copy.14
  4.2 183.0 %shard_map.104 = (bf16[96,3584]{1,0:T(8,128)(2,1)}, bf16[96,3584]{1,0:T(8,128)(2,1)}) custom-call(bf16[96,3584]{1,0:T(8,128)(2,1)} %bitcast.13, bf16[96,3584]{1,0:T(8,128)(2,1)} %bitcast.14, s32[96,8]{1,0:T(8,128)} %bitcast.18, f32[96,8]{1,0:T(8,128)} %bitcast.19, s32[96,8]{1,0:T(8,128)} %bitcast.20, f32[96,8]{1,0:T(8,128)} %bitcast.21, ...), custom_call_target="tpu_custom_call" | custom-call | tf_op jit(solution)/shard_map/pallas_call | solution.py:345
  187.2 0.0 copy-start
  187.2 2.1 %copy.17 = bf16[1,96,3584]{2,1,0:T(8,128)(2,1)} copy(bf16[1,96,3584]{2,1,0:T(8,128)(2,1)} %bitcast.16) | data formatting | bytes 1376256
  189.3 0.0 copy-done
  189.3 0.8 copy.18
Async XLA Ops:
  0.6 0.7 copy-start.1
  1.3 0.7 copy-start.2
  2.0 0.7 copy-start.3
  2.8 0.7 copy-start.4
  187.2 2.1 %copy-start = (bf16[96,3584]{1,0:T(8,128)(2,1)S(1)}, bf16[96,3584]{1,0:T(8,128)(2,1)}, u32[]{:S(2)}) copy-start(bf16[96,3584]{1,0:T(8,128)(2,1)} %get-tuple-element.5) | copy-start | bytes 2064388

commit v2 on v1

--- a/solution.py
+++ b/solution.py
@@ -19,45 +19,46 @@
     return 512 if width % 512 == 0 else 128
 
 
-def routing(ids, gates, window):
-    rows, choices = ids.shape
-    span = SUB * window
-    lane = lax.broadcasted_iota(jnp.int32, (rows, 2 * span), 1)
-    expert = lax.div(lax.rem(lane, span), SUB)
-    slot = lax.rem(lane, CAP)
-    same_half = lax.div(lane, span) == lax.div(lax.rem(lane, SUB), CAP)
-    routed = jnp.zeros((rows, 2 * span), f32)
-    gate = jnp.zeros((rows, 2 * span), f32)
-    for k in range(choices):
-        match = ids[:, k : k + 1] == expert
-        routed = jnp.where(match, 1.0, routed)
-        gate = gate + jnp.where(match, gates[:, k : k + 1], 0.0)
-    earlier = lax.broadcasted_iota(jnp.int32, (rows, rows), 1) < lax.broadcasted_iota(
-        jnp.int32, (rows, rows), 0
+def routing(ids_f, gates_f, ids_b, gates_b, window):
+    rows = ids_f.shape[1]
+    routed, gates = [], []
+    for ids, values in ((ids_f, gates_f), (ids_b, gates_b)):
+        for e in range(window):
+            match = ids == e
+            routed.append(jnp.max(jnp.where(match, 1.0, 0.0), axis=0, keepdims=True))
+            gates.append(jnp.sum(jnp.where(match, values, 0.0), axis=0, keepdims=True))
+    earlier = lax.broadcasted_iota(jnp.int32, (rows, rows), 0) < lax.broadcasted_iota(
+        jnp.int32, (rows, rows), 1
     )
     position = jnp.dot(
-        jnp.where(earlier, 1.0, 0.0).astype(bf16), routed.astype(bf16), preferred_element_type=f32
+        jnp.concatenate(routed, axis=0).astype(bf16),
+        jnp.where(earlier, 1.0, 0.0).astype(bf16),
+        preferred_element_type=f32,
     )
-    taken = (routed > 0.5) & (position == slot.astype(f32)) & same_half
-    place = jnp.where(taken, 1.0, 0.0)
-    return place, place * gate
+    slot = lax.broadcasted_iota(jnp.int32, (CAP, rows), 0).astype(f32)
+    places, weights = [], []
+    for k in range(2 * window):
+        place = jnp.where((position[k : k + 1] == slot) & (routed[k] > 0.5), 1.0, 0.0)
+        places.append(place)
+        weights.append(jnp.sum(place * gates[k], axis=1, keepdims=True))
+    return (places[:window], places[window:]), (weights[:window], weights[window:])
 
 
 def kernel(
     nsec, nx, nz,
-    x_hbm, dy_hbm, idf_ref, gf_ref, idb_ref, gb_ref, saved_hbm, up_hbm, down_hbm,
-    outf_hbm, outb_hbm,
-    xin, rows, gall, gown, upw, downw, saved, ag, rs, stage, part, plr, near, near_plr, ysend, yrecv, obuf,
-    load_sem, out_sem, xs_send, xs_recv, gs_send, gs_recv, ag_send, ag_recv, rs_send, rs_recv,
+    x_hbm, dy_hbm, idf_hbm, gf_hbm, idb_hbm, gb_hbm, saved_hbm, up_hbm, down_hbm,
+    near, near_plr, yrecv,
+    xin, ids, gates, rows, gall, gown, upw, downw, saved, ag, rs, stage, part, plr, ysend,
+    load_sem, xs_send, xs_recv, gs_send, gs_recv, ag_send, ag_recv, rs_send, rs_recv,
     near_send, near_recv, y_send, y_recv,
 ):
     half = nz // 2
-    tokens, width = xin.shape[1], xin.shape[2]
+    width = xin.shape[2]
     span = SUB * nx
     fold = width // 2
     hid = upw.shape[1] // 2
     tile = tile_of(width)
-    ftile = tile_of(fold)
+    seq = (0, 1, 3, 2) if nx == 4 else tuple(range(nx))
     early = range(nx // 2)
     late = range(nx // 2, nx)
 
@@ -84,11 +85,12 @@
         return pl.ds(pl.multiple_of(index * SUB, SUB), SUB)
 
     loads = [
-        pltpu.make_async_copy(x_hbm, xin.at[0], load_sem.at[0]),
-        pltpu.make_async_copy(dy_hbm, xin.at[1], load_sem.at[1]),
-        pltpu.make_async_copy(up_hbm, upw.at[:, pl.ds(0, hid)], load_sem.at[2]),
-        pltpu.make_async_copy(down_hbm, downw.at[pl.ds(0, hid)], load_sem.at[3]),
-        pltpu.make_async_copy(saved_hbm, saved, load_sem.at[4]),
+        pltpu.make_async_copy(src, dst, load_sem.at[k])
+        for k, (src, dst) in enumerate((
+            (idf_hbm, ids.at[0]), (gf_hbm, gates.at[0]), (idb_hbm, ids.at[1]), (gb_hbm, gates.at[1]),
+            (x_hbm, xin.at[0]), (dy_hbm, xin.at[1]),
+            (up_hbm, upw.at[:, pl.ds(0, hid)]), (down_hbm, downw.at[pl.ds(0, hid)]), (saved_hbm, saved),
+        ))
     ]
     for load in loads:
         load.start()
@@ -100,17 +102,16 @@
     for peer in peers:
         pl.semaphore_signal(barrier, inc=1, device_id=peer, device_id_type=MESH)
 
-    place_f, weight_f = routing(idf_ref[...], gf_ref[...], nx)
-    place_b, weight_b = routing(idb_ref[...], gb_ref[...], nx)
-    plr[0] = place_f.astype(bf16)
-    plr[1] = place_b.astype(bf16)
-    first = lax.broadcasted_iota(jnp.int32, place_f.shape, 1) < span
-    chosen = jnp.where(first, place_f, place_b).T.astype(bf16)
-    weight = jnp.sum(jnp.where(first, weight_f, weight_b).T, axis=1, keepdims=True)
-    gall[...] = jnp.broadcast_to(weight[:span] + weight[span:], gall.shape)
-    chosen_f, chosen_b = chosen[:span], chosen[span:]
-    loads[0].wait()
-    loads[1].wait()
+    for load in loads[:4]:
+        load.wait()
+    places, weights = routing(ids[0], gates[0], ids[1], gates[1], nx)
+    blank = jnp.zeros_like(places[0][0])
+    chosen_f = jnp.concatenate([piece for e in range(nx) for piece in (places[0][e], blank)]).astype(bf16)
+    chosen_b = jnp.concatenate([piece for e in range(nx) for piece in (blank, places[1][e])]).astype(bf16)
+    weight = jnp.concatenate([weights[h][e] for e in range(nx) for h in range(2)])
+    gall[...] = jnp.broadcast_to(weight, gall.shape)
+    for load in loads[4:6]:
+        load.wait()
 
     @pl.loop(0, width // tile)
     def _(step):
@@ -145,10 +146,10 @@
         send = ag_send.at[half if d == 0 else half + 1]
         return remote(ag.at[half - 1, d, sub(i)], ag.at[0, 1, sub(i)], send, ag_recv.at[0, 1, i], out_way[d])
 
-    for i in range(1, nx):
-        row_copy(i).start()
     for d in range(2):
         out_copy(0, d, 0, own=True).start()
+    for i in seq[1:]:
+        row_copy(i).start()
     for i in range(1, nx):
         gate_copy(i).start()
 
@@ -158,17 +159,16 @@
         for h in range(2)
         for k, (src, dst) in enumerate(((xin, near), (plr, near_plr)))
     ]
-    for copy in near_copies:
-        copy.start()
-
-    for i in range(1, nx):
+    near_copies[0].start()
+    near_copies[2].start()
+
+    for i in seq[1:]:
         row_copy(i).wait_recv()
         for d in range(2):
             out_copy(0, d, i, own=True).start()
 
-    loads[2].wait()
-    loads[3].wait()
-    loads[4].wait()
+    for load in loads[6:]:
+        load.wait()
 
     @pl.loop(0, width // tile)
     def _(step):
@@ -181,6 +181,12 @@
         value = saved[column]
         sig = jax.nn.sigmoid(value)
         saved[column] = sig * (1.0 + value * (1.0 - sig))
+
+    for h in range(2):
+        sides = [[places[h][e], blank] for e in range(nx)], [[blank, places[h][e]] for e in range(nx)]
+        spots = jnp.concatenate([piece for side in sides for pair in side for piece in pair])
+        plr[h] = spots.T.astype(bf16)
+        near_copies[2 * h + 1].start()
 
     def compute(s, sources):
         def add_up(step, total):
@@ -211,13 +217,13 @@
 
     @pl.loop(1, half - 1)
     def _(s):
-        for i in range(nx):
+        for i in seq:
             for d in range(2):
                 out_copy(s - 1, d, i).wait_recv()
                 out_copy(s, d, i).start()
         compute(s, both(s))
 
-    for i in range(nx):
+    for i in seq:
         for d in range(2):
             out_copy(half - 2, d, i).wait_recv()
             if i in (early, late)[d]:
@@ -277,19 +283,13 @@
             back_copy(1, d, i).wait_recv()
         gate = gown[sub(i), 0:1]
 
-        @pl.loop(0, fold // ftile)
-        def _(step):
-            halves = []
-            for side in range(2):
-                cols = pl.ds(pl.multiple_of(side * fold + step * ftile, 128), ftile)
-                total = part[0, 0, sub(i), cols]
-                for d in range(2):
-                    total = total + rs[0, d, sub(i), cols].astype(f32)
-                halves.append(ag[0, 0, sub(i), cols].astype(f32) + gate * total)
-            cols = pl.ds(pl.multiple_of(step * ftile, 128), ftile)
-            for h in range(2):
-                picked = [value[h * CAP : (h + 1) * CAP] for value in halves]
-                ysend[h, sub(i), cols] = jnp.concatenate(picked, axis=0).astype(bf16)
+        total = part[0, 0, sub(i)]
+        for d in range(2):
+            total = total + rs[0, d, sub(i)].astype(f32)
+        value = ag[0, 0, sub(i)].astype(f32) + gate * total
+        for h in range(2):
+            picked = value[h * CAP : (h + 1) * CAP]
+            ysend[h, sub(i)] = jnp.concatenate([picked[:, :fold], picked[:, fold:]], axis=0).astype(bf16)
 
         for h in range(2):
             y_copy(h, i).start()
@@ -299,20 +299,6 @@
     for h in range(2):
         for e in range(nx):
             remote(ysend.at[h, sub(e)], yrecv.at[h, sub(e)], y_send.at[h], y_recv.at[h, e], next_of[h]).wait_recv()
-        place = near_plr[h]
-        with_share = jnp.max(place.astype(f32), axis=1, keepdims=True) > 0.5
-        for side in range(2):
-            spots = place[:, side * span : (side + 1) * span]
-
-            @pl.loop(0, fold // ftile)
-            def _(step):
-                part_cols = pl.ds(pl.multiple_of(step * ftile, 128), ftile)
-                cols = pl.ds(pl.multiple_of(side * fold + step * ftile, 128), ftile)
-                moved = jnp.dot(spots, yrecv[h, :, part_cols], preferred_element_type=f32)
-                kept = near[h, :, cols].astype(f32)
-                obuf[h, :, cols] = jnp.where(with_share, moved, kept).astype(bf16)
-
-        pltpu.make_async_copy(obuf.at[h], (outf_hbm, outb_hbm)[h], out_sem.at[h]).start()
 
     for i in range(1, nx):
         row_copy(i).wait_send()
@@ -326,8 +312,38 @@
     remote(stage, rs.at[0, 0], rs_send.at[0], rs_recv.at[0, 0, 0], right).wait_send()
     for s in range(1, half):
         remote(rs.at[s], rs.at[s - 1], rs_send.at[s], rs_recv.at[0, 0, 0], right).wait_send()
-    for h in range(2):
-        pltpu.make_async_copy(obuf.at[h], (outf_hbm, outb_hbm)[h], out_sem.at[h]).wait()
+
+def place_rows(near, near_plr, yrecv, outf, outb, rows, places, moved, done, load_sem, out_sem):
+    width = rows.shape[2]
+    fold = width // 2
+    span = moved.shape[1]
+    first = [
+        pltpu.make_async_copy(near_plr, places, load_sem.at[0]),
+        pltpu.make_async_copy(yrecv, moved, load_sem.at[1]),
+    ]
+    sides = [(h, side, pl.ds(side * fold, fold)) for h in range(2) for side in range(2)]
+    loads = [
+        pltpu.make_async_copy(near.at[h, :, cols], rows.at[h, :, cols], load_sem.at[2 + 2 * h + side])
+        for h, side, cols in sides
+    ]
+    stores = [
+        pltpu.make_async_copy(done.at[h, :, cols], (outf, outb)[h].at[:, cols], out_sem.at[2 * h + side])
+        for h, side, cols in sides
+    ]
+    for load in first + loads:
+        load.start()
+    for load in first:
+        load.wait()
+    for (h, side, cols), load, store in zip(sides, loads, stores):
+        place = places[h]
+        with_share = jnp.max(place.astype(f32), axis=1, keepdims=True) > 0.5
+        spots = place[:, side * span : (side + 1) * span]
+        share = jnp.dot(spots, moved[h], preferred_element_type=f32)
+        load.wait()
+        done[h, :, cols] = jnp.where(with_share, share, rows[h, :, cols].astype(f32)).astype(bf16)
+        store.start()
+    for store in stores:
+        store.wait()
 
 
 def per_device(x_fwd, ids_fwd, gates_fwd, dy_bwd, ids_bwd, gates_bwd, saved_hidden, w_up, w_down):
@@ -339,16 +355,22 @@
     half = nz // 2
     tokens, width = x_fwd.shape[1:]
     span = SUB * nx
+    choices = ids_fwd.shape[2]
     any_space = pl.BlockSpec(memory_space=pl.ANY)
-    vmem = pl.BlockSpec(memory_space=pltpu.VMEM)
     dma = pltpu.SemaphoreType.DMA
-    outs = pl.pallas_call(
+    near, near_plr, yrecv = pl.pallas_call(
         functools.partial(kernel, nsec, nx, nz),
-        out_shape=[jax.ShapeDtypeStruct((tokens, width), bf16)] * 2,
-        in_specs=[any_space, any_space, vmem, vmem, vmem, vmem, any_space, any_space, any_space],
-        out_specs=[any_space, any_space],
+        out_shape=[
+            jax.ShapeDtypeStruct((2, tokens, width), bf16),
+            jax.ShapeDtypeStruct((2, tokens, 2 * span), bf16),
+            jax.ShapeDtypeStruct((2, span, width // 2), bf16),
+        ],
+        in_specs=[any_space] * 9,
+        out_specs=[any_space] * 3,
         scratch_shapes=[
             pltpu.VMEM((2, tokens, width), bf16),
+            pltpu.VMEM((2, choices, tokens), jnp.int32),
+            pltpu.VMEM((2, choices, tokens), f32),
             pltpu.VMEM((span, width), bf16),
             pltpu.VMEM((span, 128), f32),
             pltpu.VMEM((span, 128), f32),
@@ -360,12 +382,8 @@
             pltpu.VMEM((span, width), bf16),
             pltpu.VMEM((half, 2, span, width), f32),
             pltpu.VMEM((2, tokens, 2 * span), bf16),
-            pltpu.VMEM((2, tokens, width), bf16),
-            pltpu.VMEM((2, tokens, 2 * span), bf16),
             pltpu.VMEM((2, span, width // 2), bf16),
-            pltpu.VMEM((2, span, width // 2), bf16),
-            pltpu.VMEM((2, tokens, width), bf16),
-            dma((5,)), dma((2,)),
+            dma((9,)),
             dma((nx - 1,)), dma((nx - 1,)), dma((nx - 1,)), dma((nx - 1,)),
             dma((half + 2,)), dma((half, 2, nx)),
             dma((half,)), dma((half, 2, nx)),
@@ -375,9 +393,23 @@
             collective_id=0, has_side_effects=True, vmem_limit_bytes=56 * 1024 * 1024
         ),
     )(
-        x_fwd[0], dy_bwd[0], ids_fwd[0], gates_fwd[0], ids_bwd[0], gates_bwd[0],
+        x_fwd[0], dy_bwd[0], ids_fwd[0].T, gates_fwd[0].T, ids_bwd[0].T, gates_bwd[0].T,
         saved_hidden[0].reshape(nx, nz, CAP, hid), w_up[0], w_down[0],
     )
+    outs = pl.pallas_call(
+        place_rows,
+        out_shape=[jax.ShapeDtypeStruct((tokens, width), bf16)] * 2,
+        in_specs=[any_space] * 3,
+        out_specs=[any_space] * 2,
+        scratch_shapes=[
+            pltpu.VMEM((2, tokens, width), bf16),
+            pltpu.VMEM((2, tokens, 2 * span), bf16),
+            pltpu.VMEM((2, span, width // 2), bf16),
+            pltpu.VMEM((2, tokens, width), bf16),
+            dma((6,)), dma((4,)),
+        ],
+        compiler_params=pltpu.CompilerParams(vmem_limit_bytes=60 * 1024 * 1024),
+    )(near, near_plr, yrecv)
     return (outs[0][None], outs[1][None])
 
 

time: 190 us -> 177 us (0.932)
  Pallas kernels: 183 us -> 176 us
  local copies, waits for them, and re-layouts: 6.43 us -> 0 us
    pallas_call x1, Pallas kernels: 183 us -> 173 us  [per_device(): pl.pallas_call(functools.partial(kernel, nsec, nx, nz), out_shape=[jax.Sh...]
    unnamed x16 -> x0, local copies, waits for them, and re-layouts: 6.43 us -> none
    pallas_call x0 -> x1, Pallas kernels: none -> 3.26 us  [per_device(): pl.pallas_call(place_rows, out_shape=[jax.ShapeDtypeStruct((tokens, width...]
where the time goes in v2:
time: 177 us
  Pallas kernels  176 us (99%)
    pallas_call x1, Pallas kernels, per_device(): pl.pallas_call(functools.partial(kernel, nsec, nx, nz), out_shape=[jax.Sh...  173 us

profile of v2, /device:TPU:1, one launch (start us, length us, event | category | flops | bytes accessed | tf_op | source)
XLA Modules:
  0.0 176.8 jit_solution(12243882700378088287)
XLA Ops:
  0.6 172.9 %shard_map.104 = (bf16[2,96,3584]{2,1,0:T(8,128)(2,1)}, bf16[2,96,128]{2,1,0:T(8,128)(2,1)}, bf16[2,64,1792]{2,1,0:T(8,128)(2,1)}) custom-call(bf16[96,3584]{1,0:T(8,128)(2,1)} %bitcast.21, bf16[96,3584]{1,0:T(8,128)(2,1)} %bitcast.22, s32[8,96]{1,0:T(8,128)} %bitcast.24, f32[8,96]{1,0:T(8,128)} %bitcast.25, s32[8,96]{1,0:T(8,128)} %bitcast.26, ...), custom_call_target="tpu_custom_call" | custom-call | tf_op jit(solution)/shard_map/pallas_call | solution.py:361
  173.5 3.3 %shard_map.105 = (bf16[96,3584]{1,0:T(8,128)(2,1)}, bf16[96,3584]{1,0:T(8,128)(2,1)}) custom-call(bf16[2,96,3584]{2,1,0:T(8,128)(2,1)} %get-tuple-element.7.near, bf16[2,96,128]{2,1,0:T(8,128)(2,1)} %get-tuple-element.8.near_plr, bf16[2,64,1792]{2,1,0:T(8,128)(2,1)} %get-tuple-element.9.yrecv), custom_call_target="tpu_custom_call" | custom-call | tf_op jit(solution)/shard_map/pallas_call | solution.py:399

commit v3 on v2

--- a/solution.py
+++ b/solution.py
@@ -59,8 +59,8 @@
     hid = upw.shape[1] // 2
     tile = tile_of(width)
     seq = (0, 1, 3, 2) if nx == 4 else tuple(range(nx))
-    early = range(nx // 2)
-    late = range(nx // 2, nx)
+    back_seq = seq[::-1]
+    sides = (pl.ds(0, fold), pl.ds(fold, fold))
 
     sec = lax.axis_index("section")
     me = lax.axis_index("expert")
@@ -143,8 +143,8 @@
         return remote(src, ag.at[s + 1, d, sub(i)], send, ag_recv.at[s + 1, d, i], out_way[d])
 
     def far_copy(d, i):
-        send = ag_send.at[half if d == 0 else half + 1]
-        return remote(ag.at[half - 1, d, sub(i)], ag.at[0, 1, sub(i)], send, ag_recv.at[0, 1, i], out_way[d])
+        src, dst = ag.at[half - 1, d, sub(i), sides[d]], ag.at[0, 1, sub(i), sides[d]]
+        return remote(src, dst, ag_send.at[half + d], ag_recv.at[0, d, i], out_way[d])
 
     for d in range(2):
         out_copy(0, d, 0, own=True).start()
@@ -183,19 +183,22 @@
         saved[column] = sig * (1.0 + value * (1.0 - sig))
 
     for h in range(2):
-        sides = [[places[h][e], blank] for e in range(nx)], [[blank, places[h][e]] for e in range(nx)]
-        spots = jnp.concatenate([piece for side in sides for pair in side for piece in pair])
+        pairs = [[places[h][e], blank] for e in range(nx)] + [[blank, places[h][e]] for e in range(nx)]
+        spots = jnp.concatenate([piece for pair in pairs for piece in pair])
         plr[h] = spots.T.astype(bf16)
         near_copies[2 * h + 1].start()
 
-    def compute(s, sources):
+    def compute(s, first, sources):
+        count = len(sources)
+        blocks = pl.ds(first, count)
+
         def add_up(step, total):
             cols = pl.ds(pl.multiple_of(step * tile, tile), tile)
-            block = ag[s, :, :, cols].reshape(2 * span, tile)
+            block = ag[s, blocks, :, cols].reshape(count * span, tile)
             return total + jnp.dot(block, upw[cols, :], preferred_element_type=f32)
 
-        total = lax.fori_loop(0, width // tile, add_up, jnp.zeros((2 * span, 2 * hid), f32))
-        total = total.reshape(2 * nx, 2, CAP, 2 * hid)
+        total = lax.fori_loop(0, width // tile, add_up, jnp.zeros((count * span, 2 * hid), f32))
+        total = total.reshape(count * nx, 2, CAP, 2 * hid)
         forward = total[:, 0, :, :hid]
         forward = forward * jax.nn.sigmoid(forward)
         slope = jnp.stack([saved[columns[i], source] for source in sources for i in range(nx)])
@@ -204,13 +207,13 @@
         inner = jnp.stack(
             [jnp.concatenate([forward, none], axis=-1), jnp.concatenate([none, backward], axis=-1)], axis=1
         )
-        inner = inner.reshape(2 * span, 2 * hid).astype(bf16)
+        inner = inner.reshape(count * span, 2 * hid).astype(bf16)
 
         @pl.loop(0, width // tile)
         def _(step):
             cols = pl.ds(pl.multiple_of(step * tile, tile), tile)
             result = jnp.dot(inner, downw[:, cols], preferred_element_type=f32)
-            part[s, :, :, cols] = result.reshape(2, span, tile)
+            part[s, blocks, :, cols] = result.reshape(count, span, tile)
 
     def both(s):
         return (lax.rem(mz + nz - s, nz), lax.rem(mz + s, nz))
@@ -221,53 +224,57 @@
             for d in range(2):
                 out_copy(s - 1, d, i).wait_recv()
                 out_copy(s, d, i).start()
-        compute(s, both(s))
+        compute(s, 0, both(s))
 
     for i in seq:
         for d in range(2):
             out_copy(half - 2, d, i).wait_recv()
-            if i in (early, late)[d]:
-                far_copy(d, i).start()
-    compute(half - 1, both(half - 1))
+            far_copy(d, i).start()
+    compute(half - 1, 0, both(half - 1))
 
     def back_copy(s, d, i):
         return remote(
             rs.at[s, d, sub(i)], rs.at[s - 1, d, sub(i)], rs_send.at[s], rs_recv.at[s - 1, d, i], back_way[d]
         )
 
+    def half_copy(d, i, side):
+        src, dst = rs.at[half - 1, d, sub(i), sides[side]], rs.at[half - 2, d, sub(i), sides[side]]
+        return remote(src, dst, rs_send.at[half - 1], rs_recv.at[half - 2, d, i], back_way[d])
+
     def first_copy(d, i):
-        return remote(stage.at[sub(i)], rs.at[half - 1, d, sub(i)], rs_send.at[0], rs_recv.at[half - 1, d, i], back_way[d])
-
-    for d in range(2):
-        for i in (late, early)[d]:
-            rs[half - 1, d, sub(i)] = part[half - 1, d, sub(i)].astype(bf16)
-            back_copy(half - 1, d, i).start()
-    for i in range(nx):
-        far_copy(0 if i in early else 1, i).wait_recv()
-    compute(0, (mz, lax.rem(mz + half, nz)))
-    for i in range(nx):
+        src, dst = stage.at[sub(i), sides[d]], rs.at[half - 1, d, sub(i), sides[d]]
+        return remote(src, dst, rs_send.at[0], rs_recv.at[half - 1, d, i], back_way[d])
+
+    for i in back_seq:
+        for d in range(2):
+            cols = sides[1 - d]
+            rs[half - 1, d, sub(i), cols] = part[half - 1, d, sub(i), cols].astype(bf16)
+            half_copy(d, i, 1 - d).start()
+    for i in seq:
+        for d in range(2):
+            far_copy(d, i).wait_recv()
+    compute(0, 1, (lax.rem(mz + half, nz),))
+    for i in back_seq:
         stage[sub(i)] = part[0, 1, sub(i)].astype(bf16)
-        first_copy(0 if i in early else 1, i).start()
-
-    def pass_on(s, d, i):
-        rs[s, d, sub(i)] = (rs[s, d, sub(i)].astype(f32) + part[s, d, sub(i)]).astype(bf16)
-        back_copy(s, d, i).start()
-
-    for k in range(nx // 2):
-        for d in range(2):
-            i = (early, late)[d][k]
+        for d in range(2):
+            first_copy(d, i).start()
+    compute(0, 0, (mz,))
+    for i in back_seq:
+        for d in range(2):
+            cols = sides[d]
             first_copy(d, i).wait_recv()
-            pass_on(half - 1, d, i)
-
-    order = (list(late) + list(early), list(early) + list(late))
+            here = rs[half - 1, d, sub(i), cols].astype(f32) + part[half - 1, d, sub(i), cols]
+            rs[half - 1, d, sub(i), cols] = here.astype(bf16)
+            half_copy(d, i, d).start()
 
     @pl.loop(1, half - 1)
     def _(step):
         s = half - 1 - step
-        for k in range(nx):
+        for i in back_seq:
             for d in range(2):
-                back_copy(s + 1, d, order[d][k]).wait_recv()
-                pass_on(s, d, order[d][k])
+                back_copy(s + 1, d, i).wait_recv()
+                rs[s, d, sub(i)] = (rs[s, d, sub(i)].astype(f32) + part[s, d, sub(i)]).astype(bf16)
+                back_copy(s, d, i).start()
         remote(ag.at[s], ag.at[s], ag_send.at[s + 1], ag_recv.at[s, 0, 0], right).wait_send()
 
     for i in range(1, nx):
@@ -277,8 +284,7 @@
         device = ((sec_up, sec_down)[h], columns[i] * nz + mz)
         return remote(ysend.at[h, sub(i)], yrecv.at[h, sub_at(mx)], y_send.at[h], y_recv.at[h, mx], device)
 
-    for k in range(nx):
-        i = (list(early) + list(late))[(k % 2) * (nx // 2) + k // 2]
+    for i in back_seq:
         for d in range(2):
             back_copy(1, d, i).wait_recv()
         gate = gown[sub(i), 0:1]
@@ -305,43 +311,29 @@
         gate_copy(i).wait_send()
     for d in range(2):
         remote(ag.at[0, 0], ag.at[1, d], ag_send.at[d], ag_recv.at[1, d, 0], right).wait_send()
-        far_rows = pl.ds((early, late)[d][0] * SUB, SUB * (nx // 2))
-        far = ag.at[half - 1, d, far_rows]
+        far = ag.at[half - 1, d, :, sides[d]]
         remote(far, far, ag_send.at[half + d], ag_recv.at[0, 1, 0], right).wait_send()
         remote(ysend.at[d], yrecv.at[d], y_send.at[d], y_recv.at[d, 0], right).wait_send()
     remote(stage, rs.at[0, 0], rs_send.at[0], rs_recv.at[0, 0, 0], right).wait_send()
     for s in range(1, half):
         remote(rs.at[s], rs.at[s - 1], rs_send.at[s], rs_recv.at[0, 0, 0], right).wait_send()
 
-def place_rows(near, near_plr, yrecv, outf, outb, rows, places, moved, done, load_sem, out_sem):
-    width = rows.shape[2]
+def place_rows(near, places, moved, outf, outb, done, out_sem):
+    width = near.shape[2]
     fold = width // 2
     span = moved.shape[1]
-    first = [
-        pltpu.make_async_copy(near_plr, places, load_sem.at[0]),
-        pltpu.make_async_copy(yrecv, moved, load_sem.at[1]),
-    ]
-    sides = [(h, side, pl.ds(side * fold, fold)) for h in range(2) for side in range(2)]
-    loads = [
-        pltpu.make_async_copy(near.at[h, :, cols], rows.at[h, :, cols], load_sem.at[2 + 2 * h + side])
-        for h, side, cols in sides
-    ]
-    stores = [
-        pltpu.make_async_copy(done.at[h, :, cols], (outf, outb)[h].at[:, cols], out_sem.at[2 * h + side])
-        for h, side, cols in sides
-    ]
-    for load in first + loads:
-        load.start()
-    for load in first:
-        load.wait()
-    for (h, side, cols), load, store in zip(sides, loads, stores):
+    stores = []
+    for h in range(2):
         place = places[h]
         with_share = jnp.max(place.astype(f32), axis=1, keepdims=True) > 0.5
-        spots = place[:, side * span : (side + 1) * span]
-        share = jnp.dot(spots, moved[h], preferred_element_type=f32)
-        load.wait()
-        done[h, :, cols] = jnp.where(with_share, share, rows[h, :, cols].astype(f32)).astype(bf16)
-        store.start()
+        for side in range(2):
+            cols = pl.ds(side * fold, fold)
+            spots = place[:, side * span : (side + 1) * span]
+            share = jnp.dot(spots, moved[h], preferred_element_type=f32)
+            done[h, :, cols] = jnp.where(with_share, share, near[h, :, cols].astype(f32)).astype(bf16)
+            store = pltpu.make_async_copy(done.at[h, :, cols], (outf, outb)[h].at[:, cols], out_sem.at[h, side])
+            store.start()
+            stores.append(store)
     for store in stores:
         store.wait()
 
@@ -357,16 +349,17 @@
     span = SUB * nx
     choices = ids_fwd.shape[2]
     any_space = pl.BlockSpec(memory_space=pl.ANY)
+    vmem = pl.BlockSpec(memory_space=pltpu.VMEM)
     dma = pltpu.SemaphoreType.DMA
     near, near_plr, yrecv = pl.pallas_call(
         functools.partial(kernel, nsec, nx, nz),
         out_shape=[
-            jax.ShapeDtypeStruct((2, tokens, width), bf16),
-            jax.ShapeDtypeStruct((2, tokens, 2 * span), bf16),
-            jax.ShapeDtypeStruct((2, span, width // 2), bf16),
+            pltpu.VMEM((2, tokens, width), bf16),
+            pltpu.VMEM((2, tokens, 2 * span), bf16),
+            pltpu.VMEM((2, span, width // 2), bf16),
         ],
         in_specs=[any_space] * 9,
-        out_specs=[any_space] * 3,
+        out_specs=[vmem] * 3,
         scratch_shapes=[
             pltpu.VMEM((2, tokens, width), bf16),
             pltpu.VMEM((2, choices, tokens), jnp.int32),
@@ -399,17 +392,11 @@
     outs = pl.pallas_call(
         place_rows,
         out_shape=[jax.ShapeDtypeStruct((tokens, width), bf16)] * 2,
-        in_specs=[any_space] * 3,
+        in_specs=[vmem] * 3,
         out_specs=[any_space] * 2,
-        scratch_shapes=[
-            pltpu.VMEM((2, tokens, width), bf16),
-            pltpu.VMEM((2, tokens, 2 * span), bf16),
-            pltpu.VMEM((2, span, width // 2), bf16),
-            pltpu.VMEM((2, tokens, width), bf16),
-            dma((6,)), dma((4,)),
-        ],
-        compiler_params=pltpu.CompilerParams(vmem_limit_bytes=60 * 1024 * 1024),
-    )(near, near_plr, yrecv)
+        scratch_shapes=[pltpu.VMEM((2, tokens, width), bf16), dma((2, 2))],
+        compiler_params=pltpu.CompilerParams(vmem_limit_bytes=32 * 1024 * 1024),
+    )(*(pltpu.with_memory_space_constraint(v, pltpu.VMEM) for v in (near, near_plr, yrecv)))
     return (outs[0][None], outs[1][None])
 
 

time: 177 us -> 173 us (0.977)
  Pallas kernels: 176 us -> 173 us
    pallas_call x1, Pallas kernels: 3.26 us -> 1.34 us  [per_device(): pl.pallas_call(place_rows, out_shape=[jax.ShapeDtypeStruct((tokens, width...]
where the time goes in v3:
time: 173 us
  Pallas kernels  173 us (100%)
    pallas_call x1, Pallas kernels, per_device(): pl.pallas_call(functools.partial(kernel, nsec, nx, nz), out_shape=[pltpu....  171 us

profile of v3, /device:TPU:1, one launch (start us, length us, event | category | flops | bytes accessed | tf_op | source)
XLA Modules:
  0.0 173.3 jit_solution(2168715480378292942)
XLA Ops:
  0.6 171.3 %shard_map.104 = (bf16[2,96,3584]{2,1,0:T(8,128)(2,1)S(1)}, bf16[2,96,128]{2,1,0:T(8,128)(2,1)S(1)}, bf16[2,64,1792]{2,1,0:T(8,128)(2,1)S(1)}) custom-call(bf16[96,3584]{1,0:T(8,128)(2,1)} %bitcast.21, bf16[96,3584]{1,0:T(8,128)(2,1)} %bitcast.22, s32[8,96]{1,0:T(8,128)} %bitcast.24, f32[8,96]{1,0:T(8,128)} %bitcast.25, s32[8,96]{1,0:T(8,128)} %bitcast.26, ...), custom_call_target="tpu_custom_call" | custom-call | tf_op jit(solution)/shard_map/pallas_call | solution.py:354
  171.9 1.3 shard_map.105

commit v4 on v3

--- a/solution.py
+++ b/solution.py
@@ -50,7 +50,7 @@
     near, near_plr, yrecv,
     xin, ids, gates, rows, gall, gown, upw, downw, saved, ag, rs, stage, part, plr, ysend,
     load_sem, xs_send, xs_recv, gs_send, gs_recv, ag_send, ag_recv, rs_send, rs_recv,
-    near_send, near_recv, y_send, y_recv,
+    near_send, near_recv, y_send, y_recv, last_recv,
 ):
     half = nz // 2
     width = xin.shape[2]
@@ -84,6 +84,13 @@
     def sub_at(index):
         return pl.ds(pl.multiple_of(index * SUB, SUB), SUB)
 
+    peers = [right, left]
+    peers += [(sec, columns[i] * nz + mz) for i in range(1, nx)]
+    peers += [(s, columns[i] * nz + mz) for s in (sec_up, sec_down) for i in range(nx)]
+    barrier = pltpu.get_barrier_semaphore()
+    for peer in peers:
+        pl.semaphore_signal(barrier, inc=1, device_id=peer, device_id_type=MESH)
+
     loads = [
         pltpu.make_async_copy(src, dst, load_sem.at[k])
         for k, (src, dst) in enumerate((
@@ -95,13 +102,6 @@
     for load in loads:
         load.start()
 
-    peers = [right, left]
-    peers += [(sec, columns[i] * nz + mz) for i in range(1, nx)]
-    peers += [(s, columns[i] * nz + mz) for s in (sec_up, sec_down) for i in range(nx)]
-    barrier = pltpu.get_barrier_semaphore()
-    for peer in peers:
-        pl.semaphore_signal(barrier, inc=1, device_id=peer, device_id_type=MESH)
-
     for load in loads[:4]:
         load.wait()
     places, weights = routing(ids[0], gates[0], ids[1], gates[1], nx)
@@ -113,9 +113,8 @@
     for load in loads[4:6]:
         load.wait()
 
-    @pl.loop(0, width // tile)
-    def _(step):
-        cols = pl.ds(pl.multiple_of(step * tile, tile), tile)
+    for step in range(width // tile):
+        cols = pl.ds(step * tile, tile)
         rows[:, cols] = (
             jnp.dot(chosen_f, xin[0, :, cols], preferred_element_type=f32)
             + jnp.dot(chosen_b, xin[1, :, cols], preferred_element_type=f32)
@@ -125,11 +124,10 @@
     gown[sub(0)] = gall[sub_at(mx)]
     pl.semaphore_wait(barrier, len(peers))
 
-    def row_copy(i):
+    def row_copy(i, side):
         device = (sec, targets[i] * nz + mz)
-        return remote(
-            rows.at[sub_at(targets[i])], ag.at[0, 0, sub(i)], xs_send.at[i - 1], xs_recv.at[i - 1], device
-        )
+        src, dst = rows.at[sub_at(targets[i]), sides[side]], ag.at[0, 0, sub(i), sides[side]]
+        return remote(src, dst, xs_send.at[i - 1, side], xs_recv.at[i - 1, side], device)
 
     def gate_copy(i):
         device = (sec, targets[i] * nz + mz)
@@ -137,19 +135,23 @@
             gall.at[sub_at(targets[i])], gown.at[sub(i)], gs_send.at[i - 1], gs_recv.at[i - 1], device
         )
 
-    def out_copy(s, d, i, own=False):
-        src = ag.at[0, 0, sub(i)] if own else ag.at[s, d, sub(i)]
-        send = ag_send.at[d] if own else ag_send.at[s + 1]
-        return remote(src, ag.at[s + 1, d, sub(i)], send, ag_recv.at[s + 1, d, i], out_way[d])
+    def own_copy(d, i, cols):
+        src, dst = ag.at[0, 0, sub(i), cols], ag.at[1, d, sub(i), cols]
+        return remote(src, dst, ag_send.at[d], ag_recv.at[1, d, i], out_way[d])
+
+    def out_copy(s, d, i):
+        src, dst = ag.at[s, d, sub(i)], ag.at[s + 1, d, sub(i)]
+        return remote(src, dst, ag_send.at[s + 1], ag_recv.at[s + 1, d, i], out_way[d])
 
     def far_copy(d, i):
         src, dst = ag.at[half - 1, d, sub(i), sides[d]], ag.at[0, 1, sub(i), sides[d]]
         return remote(src, dst, ag_send.at[half + d], ag_recv.at[0, d, i], out_way[d])
 
     for d in range(2):
-        out_copy(0, d, 0, own=True).start()
-    for i in seq[1:]:
-        row_copy(i).start()
+        own_copy(d, 0, pl.ds(0, width)).start()
+    pieces = [(i, side) for group in (seq[1:3], seq[3:]) for side in range(2) for i in group]
+    for i, side in pieces:
+        row_copy(i, side).start()
     for i in range(1, nx):
         gate_copy(i).start()
 
@@ -162,10 +164,10 @@
     near_copies[0].start()
     near_copies[2].start()
 
-    for i in seq[1:]:
-        row_copy(i).wait_recv()
-        for d in range(2):
-            out_copy(0, d, i, own=True).start()
+    for i, side in pieces:
+        row_copy(i, side).wait_recv()
+        for d in range(2):
+            own_copy(d, i, sides[side]).start()
 
     for load in loads[6:]:
         load.wait()
@@ -267,7 +269,7 @@
             rs[half - 1, d, sub(i), cols] = here.astype(bf16)
             half_copy(d, i, d).start()
 
-    @pl.loop(1, half - 1)
+    @pl.loop(1, half - 2)
     def _(step):
         s = half - 1 - step
         for i in back_seq:
@@ -277,28 +279,45 @@
                 back_copy(s, d, i).start()
         remote(ag.at[s], ag.at[s], ag_send.at[s + 1], ag_recv.at[s, 0, 0], right).wait_send()
 
+    def last_copy(d, i, side):
+        src, dst = rs.at[1, d, sub(i), sides[side]], rs.at[0, d, sub(i), sides[side]]
+        return remote(src, dst, rs_send.at[1], last_recv.at[d, i, side], back_way[d])
+
+    for i in back_seq:
+        for d in range(2):
+            back_copy(2, d, i).wait_recv()
+        for side in range(2):
+            for d in range(2):
+                here = rs[1, d, sub(i), sides[side]].astype(f32) + part[1, d, sub(i), sides[side]]
+                rs[1, d, sub(i), sides[side]] = here.astype(bf16)
+                last_copy(d, i, side).start()
+    remote(ag.at[1], ag.at[1], ag_send.at[2], ag_recv.at[1, 0, 0], right).wait_send()
+
     for i in range(1, nx):
         gate_copy(i).wait_recv()
 
-    def y_copy(h, i):
+    quarter = fold // 2
+
+    def y_copy(h, i, side):
         device = ((sec_up, sec_down)[h], columns[i] * nz + mz)
-        return remote(ysend.at[h, sub(i)], yrecv.at[h, sub_at(mx)], y_send.at[h], y_recv.at[h, mx], device)
+        cols = pl.ds(side * quarter, quarter)
+        src, dst = ysend.at[h, sub(i), cols], yrecv.at[h, sub_at(mx), cols]
+        return remote(src, dst, y_send.at[h], y_recv.at[h, mx], device)
 
     for i in back_seq:
-        for d in range(2):
-            back_copy(1, d, i).wait_recv()
         gate = gown[sub(i), 0:1]
-
-        total = part[0, 0, sub(i)]
-        for d in range(2):
-            total = total + rs[0, d, sub(i)].astype(f32)
-        value = ag[0, 0, sub(i)].astype(f32) + gate * total
-        for h in range(2):
-            picked = value[h * CAP : (h + 1) * CAP]
-            ysend[h, sub(i)] = jnp.concatenate([picked[:, :fold], picked[:, fold:]], axis=0).astype(bf16)
-
-        for h in range(2):
-            y_copy(h, i).start()
+        for side in range(2):
+            for d in range(2):
+                last_copy(d, i, side).wait_recv()
+            total = part[0, 0, sub(i), sides[side]]
+            for d in range(2):
+                total = total + rs[0, d, sub(i), sides[side]].astype(f32)
+            value = ag[0, 0, sub(i), sides[side]].astype(f32) + gate * total
+            for h in range(2):
+                picked = value[h * CAP : (h + 1) * CAP]
+                folded = jnp.concatenate([picked[:, :quarter], picked[:, quarter:]], axis=0)
+                ysend[h, sub(i), pl.ds(side * quarter, quarter)] = folded.astype(bf16)
+                y_copy(h, i, side).start()
 
     for copy in near_copies:
         copy.wait()
@@ -307,7 +326,8 @@
             remote(ysend.at[h, sub(e)], yrecv.at[h, sub(e)], y_send.at[h], y_recv.at[h, e], next_of[h]).wait_recv()
 
     for i in range(1, nx):
-        row_copy(i).wait_send()
+        for side in range(2):
+            row_copy(i, side).wait_send()
         gate_copy(i).wait_send()
     for d in range(2):
         remote(ag.at[0, 0], ag.at[1, d], ag_send.at[d], ag_recv.at[1, d, 0], right).wait_send()
@@ -323,14 +343,18 @@
     fold = width // 2
     span = moved.shape[1]
     stores = []
+    quarter = fold // 2
     for h in range(2):
         place = places[h]
         with_share = jnp.max(place.astype(f32), axis=1, keepdims=True) > 0.5
         for side in range(2):
+            share = moved[h, :, side * quarter : (side + 1) * quarter]
+            for k in range(2):
+                cols = pl.ds((2 * side + k) * quarter, quarter)
+                spots = place[:, k * span : (k + 1) * span]
+                here = jnp.dot(spots, share, preferred_element_type=f32)
+                done[h, :, cols] = jnp.where(with_share, here, near[h, :, cols].astype(f32)).astype(bf16)
             cols = pl.ds(side * fold, fold)
-            spots = place[:, side * span : (side + 1) * span]
-            share = jnp.dot(spots, moved[h], preferred_element_type=f32)
-            done[h, :, cols] = jnp.where(with_share, share, near[h, :, cols].astype(f32)).astype(bf16)
             store = pltpu.make_async_copy(done.at[h, :, cols], (outf, outb)[h].at[:, cols], out_sem.at[h, side])
             store.start()
             stores.append(store)
@@ -377,10 +401,10 @@
             pltpu.VMEM((2, tokens, 2 * span), bf16),
             pltpu.VMEM((2, span, width // 2), bf16),
             dma((9,)),
-            dma((nx - 1,)), dma((nx - 1,)), dma((nx - 1,)), dma((nx - 1,)),
+            dma((nx - 1, 2)), dma((nx - 1, 2)), dma((nx - 1,)), dma((nx - 1,)),
             dma((half + 2,)), dma((half, 2, nx)),
             dma((half,)), dma((half, 2, nx)),
-            dma((2, 2)), dma((2, 2)), dma((2,)), dma((2, nx)),
+            dma((2, 2)), dma((2, 2)), dma((2,)), dma((2, nx)), dma((2, nx, 2)),
         ],
         compiler_params=pltpu.CompilerParams(
             collective_id=0, has_side_effects=True, vmem_limit_bytes=56 * 1024 * 1024

time: 173 us -> 171 us (0.988)
  Pallas kernels: 173 us -> 171 us
    pallas_call x1, Pallas kernels: 171 us -> 169 us  [per_device(): pl.pallas_call(functools.partial(kernel, nsec, nx, nz), out_shape=[pltpu....]
where the time goes in v4:
time: 171 us
  Pallas kernels  171 us (100%)
    pallas_call x1, Pallas kernels, per_device(): pl.pallas_call(functools.partial(kernel, nsec, nx, nz), out_shape=[pltpu....  169 us

profile of v4, /device:TPU:1, one launch (start us, length us, event | category | flops | bytes accessed | tf_op | source)
XLA Modules:
  0.0 171.2 jit_solution(3809784532273468910)
XLA Ops:
  0.6 169.2 %shard_map.104 = (bf16[2,96,3584]{2,1,0:T(8,128)(2,1)S(1)}, bf16[2,96,128]{2,1,0:T(8,128)(2,1)S(1)}, bf16[2,64,1792]{2,1,0:T(8,128)(2,1)S(1)}) custom-call(bf16[96,3584]{1,0:T(8,128)(2,1)} %bitcast.21, bf16[96,3584]{1,0:T(8,128)(2,1)} %bitcast.22, s32[8,96]{1,0:T(8,128)} %bitcast.24, f32[8,96]{1,0:T(8,128)} %bitcast.25, s32[8,96]{1,0:T(8,128)} %bitcast.26, ...), custom_call_target="tpu_custom_call" | custom-call | tf_op jit(solution)/shard_map/pallas_call | solution.py:378
  169.9 1.4 shard_map.105

commit v5 on v4

--- a/solution.py
+++ b/solution.py
@@ -1,4 +1,5 @@
 import functools
+import math
 
 import jax
 import jax.numpy as jnp
@@ -11,8 +12,12 @@
 CAP = 8
 SUB = 2 * CAP
 FF = 2048
+TOP_CODE = 32000.0
+LEVELS = 256 / math.log(2)
 f32 = jnp.float32
 bf16 = jnp.bfloat16
+i32 = jnp.int32
+i16 = jnp.int16
 
 
 def tile_of(width):
@@ -27,15 +32,15 @@
             match = ids == e
             routed.append(jnp.max(jnp.where(match, 1.0, 0.0), axis=0, keepdims=True))
             gates.append(jnp.sum(jnp.where(match, values, 0.0), axis=0, keepdims=True))
-    earlier = lax.broadcasted_iota(jnp.int32, (rows, rows), 0) < lax.broadcasted_iota(
-        jnp.int32, (rows, rows), 1
+    earlier = lax.broadcasted_iota(i32, (rows, rows), 0) < lax.broadcasted_iota(
+        i32, (rows, rows), 1
     )
     position = jnp.dot(
         jnp.concatenate(routed, axis=0).astype(bf16),
         jnp.where(earlier, 1.0, 0.0).astype(bf16),
         preferred_element_type=f32,
     )
-    slot = lax.broadcasted_iota(jnp.int32, (CAP, rows), 0).astype(f32)
+    slot = lax.broadcasted_iota(i32, (CAP, rows), 0).astype(f32)
     places, weights = [], []
     for k in range(2 * window):
         place = jnp.where((position[k : k + 1] == slot) & (routed[k] > 0.5), 1.0, 0.0)
@@ -61,6 +66,10 @@
     seq = (0, 1, 3, 2) if nx == 4 else tuple(range(nx))
     back_seq = seq[::-1]
     sides = (pl.ds(0, fold), pl.ds(fold, fold))
+    code_cols = (pl.ds(0, fold), pl.ds(fold + 128, fold))
+    level_cols = (pl.ds(fold, 128), pl.ds(width + 128, 128))
+    wire_sides = (pl.ds(0, fold + 128), pl.ds(fold + 128, fold + 128))
+    wire_whole = pl.ds(0, width + 128)
 
     sec = lax.axis_index("section")
     me = lax.axis_index("expert")
@@ -215,7 +224,7 @@
         def _(step):
             cols = pl.ds(pl.multiple_of(step * tile, tile), tile)
             result = jnp.dot(inner, downw[:, cols], preferred_element_type=f32)
-            part[s, blocks, :, cols] = result.reshape(count, span, tile)
+            part[s, blocks, :, cols] = result.reshape(count, span, tile).astype(bf16)
 
     def both(s):
         return (lax.rem(mz + nz - s, nz), lax.rem(mz + s, nz))
@@ -234,64 +243,109 @@
             far_copy(d, i).start()
     compute(half - 1, 0, both(half - 1))
 
+    def top_of(value):
+        return jnp.max(jnp.abs(value), axis=1, keepdims=True)
+
+    def level_of(top):
+        return jnp.ceil(jnp.log(jnp.maximum(top, 1e-30) * (1.0 / TOP_CODE)) * LEVELS)
+
+    def write(ref, i, side, value, level):
+        codes = jnp.round(value * jnp.exp(level * (-1.0 / LEVELS)))
+        ref[sub(i), code_cols[side]] = codes.astype(i32).astype(i16)
+
+    def mark(ref, i, side, level):
+        ref[sub(i), level_cols[side]] = jnp.broadcast_to(level, (SUB, 128)).astype(i32).astype(i16)
+
+    def write_half(ref, i, side, value):
+        level = level_of(top_of(value))
+        write(ref, i, side, value, level)
+        mark(ref, i, side, level)
+
+    def write_whole(ref, i, values):
+        level = level_of(jnp.maximum(top_of(values[0]), top_of(values[1])))
+        for side in range(2):
+            write(ref, i, side, values[side], level)
+        mark(ref, i, 0, level)
+
+    def read(ref, i, side, mark_side):
+        level = ref[sub(i), level_cols[mark_side]].astype(i32).astype(f32)[:, :1]
+        return ref[sub(i), code_cols[side]].astype(i32).astype(f32) * jnp.exp(level * (1.0 / LEVELS))
+
+    def term(s, d, i, side):
+        return part[s, d, sub(i), sides[side]].astype(f32)
+
     def back_copy(s, d, i):
-        return remote(
-            rs.at[s, d, sub(i)], rs.at[s - 1, d, sub(i)], rs_send.at[s], rs_recv.at[s - 1, d, i], back_way[d]
-        )
+        src, dst = rs.at[s, d, sub(i), wire_whole], rs.at[s - 1, d, sub(i), wire_whole]
+        return remote(src, dst, rs_send.at[s], rs_recv.at[s - 1, d, i], back_way[d])
 
     def half_copy(d, i, side):
-        src, dst = rs.at[half - 1, d, sub(i), sides[side]], rs.at[half - 2, d, sub(i), sides[side]]
+        src, dst = rs.at[half - 1, d, sub(i), wire_sides[side]], rs.at[half - 2, d, sub(i), wire_sides[side]]
         return remote(src, dst, rs_send.at[half - 1], rs_recv.at[half - 2, d, i], back_way[d])
 
+    def both_halves(d, i):
+        src, dst = rs.at[half - 1, d, sub(i)], rs.at[half - 2, d, sub(i)]
+        return remote(src, dst, rs_send.at[half - 1], rs_recv.at[half - 2, d, i], back_way[d])
+
     def first_copy(d, i):
-        src, dst = stage.at[sub(i), sides[d]], rs.at[half - 1, d, sub(i), sides[d]]
+        src, dst = stage.at[sub(i), wire_sides[d]], rs.at[half - 1, d, sub(i), wire_sides[d]]
         return remote(src, dst, rs_send.at[0], rs_recv.at[half - 1, d, i], back_way[d])
 
+    def last_copy(d, i, side):
+        src, dst = rs.at[1, d, sub(i), wire_sides[side]], rs.at[0, d, sub(i), wire_sides[side]]
+        return remote(src, dst, rs_send.at[1], last_recv.at[d, i, side], back_way[d])
+
     for i in back_seq:
         for d in range(2):
-            cols = sides[1 - d]
-            rs[half - 1, d, sub(i), cols] = part[half - 1, d, sub(i), cols].astype(bf16)
+            write_half(rs.at[half - 1, d], i, 1 - d, term(half - 1, d, i, 1 - d))
             half_copy(d, i, 1 - d).start()
     for i in seq:
         for d in range(2):
             far_copy(d, i).wait_recv()
     compute(0, 1, (lax.rem(mz + half, nz),))
     for i in back_seq:
-        stage[sub(i)] = part[0, 1, sub(i)].astype(bf16)
-        for d in range(2):
+        for d in range(2):
+            write_half(stage, i, d, term(0, 1, i, d))
             first_copy(d, i).start()
     compute(0, 0, (mz,))
     for i in back_seq:
         for d in range(2):
-            cols = sides[d]
             first_copy(d, i).wait_recv()
-            here = rs[half - 1, d, sub(i), cols].astype(f32) + part[half - 1, d, sub(i), cols]
-            rs[half - 1, d, sub(i), cols] = here.astype(bf16)
+            ref = rs.at[half - 1, d]
+            write_half(ref, i, d, read(ref, i, d, d) + term(half - 1, d, i, d))
             half_copy(d, i, d).start()
 
-    @pl.loop(1, half - 2)
+    def pass_on(s, d, i, marks):
+        ref = rs.at[s, d]
+        write_whole(ref, i, [read(ref, i, side, marks[side]) + term(s, d, i, side) for side in range(2)])
+        back_copy(s, d, i).start()
+
+    def settle(s):
+        remote(ag.at[s], ag.at[s], ag_send.at[s + 1], ag_recv.at[s, 0, 0], right).wait_send()
+
+    for i in back_seq:
+        for d in range(2):
+            both_halves(d, i).wait_recv()
+            pass_on(half - 2, d, i, (0, 1))
+    settle(half - 2)
+
+    @pl.loop(1, half - 3)
     def _(step):
-        s = half - 1 - step
+        s = half - 2 - step
         for i in back_seq:
             for d in range(2):
                 back_copy(s + 1, d, i).wait_recv()
-                rs[s, d, sub(i)] = (rs[s, d, sub(i)].astype(f32) + part[s, d, sub(i)]).astype(bf16)
-                back_copy(s, d, i).start()
-        remote(ag.at[s], ag.at[s], ag_send.at[s + 1], ag_recv.at[s, 0, 0], right).wait_send()
-
-    def last_copy(d, i, side):
-        src, dst = rs.at[1, d, sub(i), sides[side]], rs.at[0, d, sub(i), sides[side]]
-        return remote(src, dst, rs_send.at[1], last_recv.at[d, i, side], back_way[d])
+                pass_on(s, d, i, (0, 0))
+        settle(s)
 
     for i in back_seq:
         for d in range(2):
             back_copy(2, d, i).wait_recv()
+        sums = [[read(rs.at[1, d], i, side, 0) + term(1, d, i, side) for d in range(2)] for side in range(2)]
         for side in range(2):
             for d in range(2):
-                here = rs[1, d, sub(i), sides[side]].astype(f32) + part[1, d, sub(i), sides[side]]
-                rs[1, d, sub(i), sides[side]] = here.astype(bf16)
+                write_half(rs.at[1, d], i, side, sums[side][d])
                 last_copy(d, i, side).start()
-    remote(ag.at[1], ag.at[1], ag_send.at[2], ag_recv.at[1, 0, 0], right).wait_send()
+    settle(1)
 
     for i in range(1, nx):
         gate_copy(i).wait_recv()
@@ -303,27 +357,6 @@
         cols = pl.ds(side * quarter, quarter)
         src, dst = ysend.at[h, sub(i), cols], yrecv.at[h, sub_at(mx), cols]
         return remote(src, dst, y_send.at[h], y_recv.at[h, mx], device)
-
-    for i in back_seq:
-        gate = gown[sub(i), 0:1]
-        for side in range(2):
-            for d in range(2):
-                last_copy(d, i, side).wait_recv()
-            total = part[0, 0, sub(i), sides[side]]
-            for d in range(2):
-                total = total + rs[0, d, sub(i), sides[side]].astype(f32)
-            value = ag[0, 0, sub(i), sides[side]].astype(f32) + gate * total
-            for h in range(2):
-                picked = value[h * CAP : (h + 1) * CAP]
-                folded = jnp.concatenate([picked[:, :quarter], picked[:, quarter:]], axis=0)
-                ysend[h, sub(i), pl.ds(side * quarter, quarter)] = folded.astype(bf16)
-                y_copy(h, i, side).start()
-
-    for copy in near_copies:
-        copy.wait()
-    for h in range(2):
-        for e in range(nx):
-            remote(ysend.at[h, sub(e)], yrecv.at[h, sub(e)], y_send.at[h], y_recv.at[h, e], next_of[h]).wait_recv()
 
     for i in range(1, nx):
         for side in range(2):
@@ -333,10 +366,36 @@
         remote(ag.at[0, 0], ag.at[1, d], ag_send.at[d], ag_recv.at[1, d, 0], right).wait_send()
         far = ag.at[half - 1, d, :, sides[d]]
         remote(far, far, ag_send.at[half + d], ag_recv.at[0, 1, 0], right).wait_send()
+    remote(stage, rs.at[0, 0], rs_send.at[0], rs_recv.at[0, 0, 0], right).wait_send()
+    for s in range(2, half):
+        sent = rs.at[s, :, :, wire_whole] if s < half - 1 else rs.at[s]
+        remote(sent, sent, rs_send.at[s], rs_recv.at[0, 0, 0], right).wait_send()
+    for copy in near_copies:
+        copy.wait()
+
+    for i in back_seq:
+        gate = gown[sub(i), 0:1]
+        for side in range(2):
+            for d in range(2):
+                last_copy(d, i, side).wait_recv()
+            total = term(0, 0, i, side)
+            for d in range(2):
+                total = total + read(rs.at[0, d], i, side, side)
+            value = ag[0, 0, sub(i), sides[side]].astype(f32) + gate * total
+            for h in range(2):
+                picked = value[h * CAP : (h + 1) * CAP]
+                folded = jnp.concatenate([picked[:, :quarter], picked[:, quarter:]], axis=0)
+                ysend[h, sub(i), pl.ds(side * quarter, quarter)] = folded.astype(bf16)
+                y_copy(h, i, side).start()
+
+    for h in range(2):
+        for e in range(nx):
+            remote(ysend.at[h, sub(e)], yrecv.at[h, sub(e)], y_send.at[h], y_recv.at[h, e], next_of[h]).wait_recv()
+
+    for d in range(2):
         remote(ysend.at[d], yrecv.at[d], y_send.at[d], y_recv.at[d, 0], right).wait_send()
-    remote(stage, rs.at[0, 0], rs_send.at[0], rs_recv.at[0, 0, 0], right).wait_send()
-    for s in range(1, half):
-        remote(rs.at[s], rs.at[s - 1], rs_send.at[s], rs_recv.at[0, 0, 0], right).wait_send()
+    remote(rs.at[1], rs.at[0], rs_send.at[1], rs_recv.at[0, 0, 0], right).wait_send()
+
 
 def place_rows(near, places, moved, outf, outb, done, out_sem):
     width = near.shape[2]
@@ -386,7 +445,7 @@
         out_specs=[vmem] * 3,
         scratch_shapes=[
             pltpu.VMEM((2, tokens, width), bf16),
-            pltpu.VMEM((2, choices, tokens), jnp.int32),
+            pltpu.VMEM((2, choices, tokens), i32),
             pltpu.VMEM((2, choices, tokens), f32),
             pltpu.VMEM((span, width), bf16),
             pltpu.VMEM((span, 128), f32),
@@ -395,9 +454,9 @@
             pltpu.VMEM((2 * hid, width), bf16),
             pltpu.VMEM((nx, nz, CAP, hid), f32),
             pltpu.VMEM((half, 2, span, width), bf16),
+            pltpu.VMEM((half, 2, span, width + 256), i16),
+            pltpu.VMEM((span, width + 256), i16),
             pltpu.VMEM((half, 2, span, width), bf16),
-            pltpu.VMEM((span, width), bf16),
-            pltpu.VMEM((half, 2, span, width), f32),
             pltpu.VMEM((2, tokens, 2 * span), bf16),
             pltpu.VMEM((2, span, width // 2), bf16),
             dma((9,)),

time: 171 us -> 175 us (1.023)
  Pallas kernels: 171 us -> 174 us
    pallas_call x1, Pallas kernels: 169 us -> 173 us  [per_device(): pl.pallas_call(functools.partial(kernel, nsec, nx, nz), out_shape=[pltpu....]
where the time goes in v5:
time: 175 us
  Pallas kernels  174 us (99%)
    pallas_call x1, Pallas kernels, per_device(): pl.pallas_call(functools.partial(kernel, nsec, nx, nz), out_shape=[pltpu....  173 us

profile of v5, /device:TPU:1, one launch (start us, length us, event | category | flops | bytes accessed | tf_op | source)
XLA Modules:
  0.0 174.8 jit_solution(11018118121813146815)
XLA Ops:
  0.6 172.8 %shard_map.104 = (bf16[2,96,3584]{2,1,0:T(8,128)(2,1)S(1)}, bf16[2,96,128]{2,1,0:T(8,128)(2,1)S(1)}, bf16[2,64,1792]{2,1,0:T(8,128)(2,1)S(1)}) custom-call(bf16[96,3584]{1,0:T(8,128)(2,1)} %bitcast.21, bf16[96,3584]{1,0:T(8,128)(2,1)} %bitcast.22, s32[8,96]{1,0:T(8,128)} %bitcast.24, f32[8,96]{1,0:T(8,128)} %bitcast.25, s32[8,96]{1,0:T(8,128)} %bitcast.26, ...), custom_call_target="tpu_custom_call" | custom-call | tf_op jit(solution)/shard_map/pallas_call | solution.py:437
  173.4 1.4 shard_map.105

commit v6 on v5

--- a/solution.py
+++ b/solution.py
@@ -53,9 +53,10 @@
     nsec, nx, nz,
     x_hbm, dy_hbm, idf_hbm, gf_hbm, idb_hbm, gb_hbm, saved_hbm, up_hbm, down_hbm,
     near, near_plr, yrecv,
+    level_in, level_out, bound,
     xin, ids, gates, rows, gall, gown, upw, downw, saved, ag, rs, stage, part, plr, ysend,
     load_sem, xs_send, xs_recv, gs_send, gs_recv, ag_send, ag_recv, rs_send, rs_recv,
-    near_send, near_recv, y_send, y_recv, last_recv,
+    near_send, near_recv, y_send, y_recv, last_recv, lv_send, lv_recv,
 ):
     half = nz // 2
     width = xin.shape[2]
@@ -66,10 +67,7 @@
     seq = (0, 1, 3, 2) if nx == 4 else tuple(range(nx))
     back_seq = seq[::-1]
     sides = (pl.ds(0, fold), pl.ds(fold, fold))
-    code_cols = (pl.ds(0, fold), pl.ds(fold + 128, fold))
-    level_cols = (pl.ds(fold, 128), pl.ds(width + 128, 128))
-    wire_sides = (pl.ds(0, fold + 128), pl.ds(fold + 128, fold + 128))
-    wire_whole = pl.ds(0, width + 128)
+    group = 128 // nx
 
     sec = lax.axis_index("section")
     me = lax.axis_index("expert")
@@ -220,11 +218,24 @@
         )
         inner = inner.reshape(count * span, 2 * hid).astype(bf16)
 
-        @pl.loop(0, width // tile)
-        def _(step):
+        def take_down(step, top):
             cols = pl.ds(pl.multiple_of(step * tile, tile), tile)
-            result = jnp.dot(inner, downw[:, cols], preferred_element_type=f32)
-            part[s, blocks, :, cols] = result.reshape(count, span, tile).astype(bf16)
+            result = jnp.dot(inner, downw[:, cols], preferred_element_type=f32).astype(bf16)
+            part[s, blocks, :, cols] = result.reshape(count, span, tile)
+            size = jnp.abs(result.astype(f32))
+            for k in range(tile // 128):
+                top = jnp.maximum(top, size[:, k * 128 : (k + 1) * 128])
+            return top
+
+        top = lax.fori_loop(0, width // tile, take_down, jnp.zeros((count * span, 128), f32))
+        top = jnp.max(top, axis=1, keepdims=True)
+        lane_group = lax.div(lax.broadcasted_iota(i32, (SUB, 128), 1), group)
+        for k in range(count):
+            spread = jnp.zeros((SUB, 128), f32)
+            for i in range(nx):
+                start = k * span + i * SUB
+                spread = jnp.where(lane_group == i, top[start : start + SUB], spread)
+            bound[s, first + k] = spread
 
     def both(s):
         return (lax.rem(mz + nz - s, nz), lax.rem(mz + s, nz))
@@ -243,107 +254,117 @@
             far_copy(d, i).start()
     compute(half - 1, 0, both(half - 1))
 
-    def top_of(value):
-        return jnp.max(jnp.abs(value), axis=1, keepdims=True)
-
-    def level_of(top):
-        return jnp.ceil(jnp.log(jnp.maximum(top, 1e-30) * (1.0 / TOP_CODE)) * LEVELS)
-
-    def write(ref, i, side, value, level):
-        codes = jnp.round(value * jnp.exp(level * (-1.0 / LEVELS)))
-        ref[sub(i), code_cols[side]] = codes.astype(i32).astype(i16)
-
-    def mark(ref, i, side, level):
-        ref[sub(i), level_cols[side]] = jnp.broadcast_to(level, (SUB, 128)).astype(i32).astype(i16)
-
-    def write_half(ref, i, side, value):
-        level = level_of(top_of(value))
-        write(ref, i, side, value, level)
-        mark(ref, i, side, level)
-
-    def write_whole(ref, i, values):
-        level = level_of(jnp.maximum(top_of(values[0]), top_of(values[1])))
-        for side in range(2):
-            write(ref, i, side, values[side], level)
-        mark(ref, i, 0, level)
-
-    def read(ref, i, side, mark_side):
-        level = ref[sub(i), level_cols[mark_side]].astype(i32).astype(f32)[:, :1]
-        return ref[sub(i), code_cols[side]].astype(i32).astype(f32) * jnp.exp(level * (1.0 / LEVELS))
+    def level_copy(k, to, d):
+        return remote(level_out.at[k, d], level_in.at[to, d], lv_send.at[k, d], lv_recv.at[to, d], back_way[d])
+
+    def bound_in(k, d):
+        return TOP_CODE * jnp.exp(level_in[k, d].astype(i32).astype(f32) * (1.0 / LEVELS))
+
+    def send_level(k, to, d, most):
+        level = jnp.ceil(jnp.log(jnp.maximum(most, 1e-30) * (1.0 / TOP_CODE)) * LEVELS)
+        level_out[k, d] = level.astype(i32).astype(i16)
+        level_copy(k, to, d).start()
+
+    def level_of(ref, k, d, i):
+        return ref[k, d].astype(i32).astype(f32)[:, i * group : i * group + 1]
+
+    def write(ref, i, side, value, k, d):
+        codes = jnp.round(value * jnp.exp(level_of(level_out, k, d, i) * (-1.0 / LEVELS)))
+        ref[sub(i), sides[side]] = codes.astype(i32).astype(i16)
+
+    def read(ref, i, side, k, d):
+        codes = ref[sub(i), sides[side]].astype(i32).astype(f32)
+        return codes * jnp.exp(level_of(level_in, k, d, i) * (1.0 / LEVELS))
 
     def term(s, d, i, side):
         return part[s, d, sub(i), sides[side]].astype(f32)
 
     def back_copy(s, d, i):
-        src, dst = rs.at[s, d, sub(i), wire_whole], rs.at[s - 1, d, sub(i), wire_whole]
+        src, dst = rs.at[s, d, sub(i)], rs.at[s - 1, d, sub(i)]
         return remote(src, dst, rs_send.at[s], rs_recv.at[s - 1, d, i], back_way[d])
 
     def half_copy(d, i, side):
-        src, dst = rs.at[half - 1, d, sub(i), wire_sides[side]], rs.at[half - 2, d, sub(i), wire_sides[side]]
+        src, dst = rs.at[half - 1, d, sub(i), sides[side]], rs.at[half - 2, d, sub(i), sides[side]]
         return remote(src, dst, rs_send.at[half - 1], rs_recv.at[half - 2, d, i], back_way[d])
 
-    def both_halves(d, i):
-        src, dst = rs.at[half - 1, d, sub(i)], rs.at[half - 2, d, sub(i)]
-        return remote(src, dst, rs_send.at[half - 1], rs_recv.at[half - 2, d, i], back_way[d])
-
     def first_copy(d, i):
-        src, dst = stage.at[sub(i), wire_sides[d]], rs.at[half - 1, d, sub(i), wire_sides[d]]
+        src, dst = stage.at[sub(i), sides[d]], rs.at[half - 1, d, sub(i), sides[d]]
         return remote(src, dst, rs_send.at[0], rs_recv.at[half - 1, d, i], back_way[d])
 
     def last_copy(d, i, side):
-        src, dst = rs.at[1, d, sub(i), wire_sides[side]], rs.at[0, d, sub(i), wire_sides[side]]
+        src, dst = rs.at[1, d, sub(i), sides[side]], rs.at[0, d, sub(i), sides[side]]
         return remote(src, dst, rs_send.at[1], last_recv.at[d, i, side], back_way[d])
 
+    for d in range(2):
+        send_level(half, half, d, bound[half - 1, d])
     for i in back_seq:
         for d in range(2):
-            write_half(rs.at[half - 1, d], i, 1 - d, term(half - 1, d, i, 1 - d))
+            write(rs.at[half - 1, d], i, 1 - d, term(half - 1, d, i, 1 - d), half, d)
             half_copy(d, i, 1 - d).start()
     for i in seq:
         for d in range(2):
             far_copy(d, i).wait_recv()
     compute(0, 1, (lax.rem(mz + half, nz),))
+    for d in range(2):
+        send_level(0, half - 1, d, bound[0, 1])
     for i in back_seq:
         for d in range(2):
-            write_half(stage, i, d, term(0, 1, i, d))
+            write(stage, i, d, term(0, 1, i, d), 0, d)
             first_copy(d, i).start()
     compute(0, 0, (mz,))
+    for d in range(2):
+        level_copy(0, half - 1, d).wait_recv()
+        send_level(half - 1, half - 2, d, bound_in(half - 1, d) + bound[half - 1, d])
     for i in back_seq:
         for d in range(2):
             first_copy(d, i).wait_recv()
             ref = rs.at[half - 1, d]
-            write_half(ref, i, d, read(ref, i, d, d) + term(half - 1, d, i, d))
+            write(ref, i, d, read(ref, i, d, half - 1, d) + term(half - 1, d, i, d), half - 1, d)
             half_copy(d, i, d).start()
-
-    def pass_on(s, d, i, marks):
-        ref = rs.at[s, d]
-        write_whole(ref, i, [read(ref, i, side, marks[side]) + term(s, d, i, side) for side in range(2)])
-        back_copy(s, d, i).start()
 
     def settle(s):
         remote(ag.at[s], ag.at[s], ag_send.at[s + 1], ag_recv.at[s, 0, 0], right).wait_send()
 
+    for d in range(2):
+        level_copy(half, half, d).wait_recv()
+        level_copy(half - 1, half - 2, d).wait_recv()
+        most = jnp.maximum(bound_in(half, d), bound_in(half - 2, d))
+        send_level(half - 2, half - 3, d, most + bound[half - 2, d])
     for i in back_seq:
         for d in range(2):
-            both_halves(d, i).wait_recv()
-            pass_on(half - 2, d, i, (0, 1))
+            back_copy(half - 1, d, i).wait_recv()
+            ref = rs.at[half - 2, d]
+            for side in range(2):
+                level = half - 2 if side == d else half
+                write(ref, i, side, read(ref, i, side, level, d) + term(half - 2, d, i, side), half - 2, d)
+            back_copy(half - 2, d, i).start()
     settle(half - 2)
 
     @pl.loop(1, half - 3)
     def _(step):
         s = half - 2 - step
+        for d in range(2):
+            level_copy(s + 1, s, d).wait_recv()
+            send_level(s, s - 1, d, bound_in(s, d) + bound[s, d])
         for i in back_seq:
             for d in range(2):
                 back_copy(s + 1, d, i).wait_recv()
-                pass_on(s, d, i, (0, 0))
+                ref = rs.at[s, d]
+                for side in range(2):
+                    write(ref, i, side, read(ref, i, side, s, d) + term(s, d, i, side), s, d)
+                back_copy(s, d, i).start()
         settle(s)
 
+    for d in range(2):
+        level_copy(2, 1, d).wait_recv()
+        send_level(1, 0, d, bound_in(1, d) + bound[1, d])
     for i in back_seq:
         for d in range(2):
             back_copy(2, d, i).wait_recv()
-        sums = [[read(rs.at[1, d], i, side, 0) + term(1, d, i, side) for d in range(2)] for side in range(2)]
         for side in range(2):
             for d in range(2):
-                write_half(rs.at[1, d], i, side, sums[side][d])
+                ref = rs.at[1, d]
+                write(ref, i, side, read(ref, i, side, 1, d) + term(1, d, i, side), 1, d)
                 last_copy(d, i, side).start()
     settle(1)
 
@@ -368,8 +389,11 @@
         remote(far, far, ag_send.at[half + d], ag_recv.at[0, 1, 0], right).wait_send()
     remote(stage, rs.at[0, 0], rs_send.at[0], rs_recv.at[0, 0, 0], right).wait_send()
     for s in range(2, half):
-        sent = rs.at[s, :, :, wire_whole] if s < half - 1 else rs.at[s]
-        remote(sent, sent, rs_send.at[s], rs_recv.at[0, 0, 0], right).wait_send()
+        remote(rs.at[s], rs.at[s - 1], rs_send.at[s], rs_recv.at[0, 0, 0], right).wait_send()
+    for d in range(2):
+        level_copy(1, 0, d).wait()
+        for k in (0, *range(2, half + 1)):
+            level_copy(k, 0, d).wait_send()
     for copy in near_copies:
         copy.wait()
 
@@ -380,7 +404,7 @@
                 last_copy(d, i, side).wait_recv()
             total = term(0, 0, i, side)
             for d in range(2):
-                total = total + read(rs.at[0, d], i, side, side)
+                total = total + read(rs.at[0, d], i, side, 0, d)
             value = ag[0, 0, sub(i), sides[side]].astype(f32) + gate * total
             for h in range(2):
                 picked = value[h * CAP : (h + 1) * CAP]
@@ -444,6 +468,9 @@
         in_specs=[any_space] * 9,
         out_specs=[vmem] * 3,
         scratch_shapes=[
+            pltpu.VMEM((half + 1, 2, SUB, 128), i16),
+            pltpu.VMEM((half + 1, 2, SUB, 128), i16),
+            pltpu.VMEM((half, 2, SUB, 128), f32),
             pltpu.VMEM((2, tokens, width), bf16),
             pltpu.VMEM((2, choices, tokens), i32),
             pltpu.VMEM((2, choices, tokens), f32),
@@ -454,8 +481,8 @@
             pltpu.VMEM((2 * hid, width), bf16),
             pltpu.VMEM((nx, nz, CAP, hid), f32),
             pltpu.VMEM((half, 2, span, width), bf16),
-            pltpu.VMEM((half, 2, span, width + 256), i16),
-            pltpu.VMEM((span, width + 256), i16),
+            pltpu.VMEM((half, 2, span, width), i16),
+            pltpu.VMEM((span, width), i16),
             pltpu.VMEM((half, 2, span, width), bf16),
             pltpu.VMEM((2, tokens, 2 * span), bf16),
             pltpu.VMEM((2, span, width // 2), bf16),
@@ -463,7 +490,7 @@
             dma((nx - 1, 2)), dma((nx - 1, 2)), dma((nx - 1,)), dma((nx - 1,)),
             dma((half + 2,)), dma((half, 2, nx)),
             dma((half,)), dma((half, 2, nx)),
-            dma((2, 2)), dma((2, 2)), dma((2,)), dma((2, nx)), dma((2, nx, 2)),
+            dma((2, 2)), dma((2, 2)), dma((2,)), dma((2, nx)), dma((2, nx, 2)), dma((half + 1, 2)), dma((half + 1, 2)),
         ],
         compiler_params=pltpu.CompilerParams(
             collective_id=0, has_side_effects=True, vmem_limit_bytes=56 * 1024 * 1024

time: 175 us -> 173 us (0.989)
  Pallas kernels: 174 us -> 172 us
    pallas_call x1, Pallas kernels: 173 us -> 170 us  [per_device(): pl.pallas_call(functools.partial(kernel, nsec, nx, nz), out_shape=[pltpu....]
where the time goes in v6:
time: 173 us; the launch traced here: 172 us
  Pallas kernels  172 us (99%)
    pallas_call x1, Pallas kernels, per_device(): pl.pallas_call(functools.partial(kernel, nsec, nx, nz), out_shape=[pltpu....  170 us

profile of v6, /device:TPU:1, one launch (start us, length us, event | category | flops | bytes accessed | tf_op | source)
XLA Modules:
  0.0 172.4 jit_solution(17284812495044084593)
XLA Ops:
  0.6 170.4 %shard_map.104 = (bf16[2,96,3584]{2,1,0:T(8,128)(2,1)S(1)}, bf16[2,96,128]{2,1,0:T(8,128)(2,1)S(1)}, bf16[2,64,1792]{2,1,0:T(8,128)(2,1)S(1)}) custom-call(bf16[96,3584]{1,0:T(8,128)(2,1)} %bitcast.21, bf16[96,3584]{1,0:T(8,128)(2,1)} %bitcast.22, s32[8,96]{1,0:T(8,128)} %bitcast.24, f32[8,96]{1,0:T(8,128)} %bitcast.25, s32[8,96]{1,0:T(8,128)} %bitcast.26, ...), custom_call_target="tpu_custom_call" | custom-call | tf_op jit(solution)/shard_map/pallas_call | solution.py:461
  171.1 1.4 shard_map.105

commit v7 on v6

--- a/solution.py
+++ b/solution.py
@@ -66,7 +66,10 @@
     tile = tile_of(width)
     seq = (0, 1, 3, 2) if nx == 4 else tuple(range(nx))
     back_seq = seq[::-1]
+    twos = range(nx // 2)
     sides = (pl.ds(0, fold), pl.ds(fold, fold))
+    quarter = fold // 2
+    quarters = [pl.ds(k * quarter, quarter) for k in range(4)]
     group = 128 // nx
 
     sec = lax.axis_index("section")
@@ -88,6 +91,9 @@
     def sub(i):
         return pl.ds(i * SUB, SUB)
 
+    def pair(p):
+        return pl.ds(p * 2 * SUB, 2 * SUB)
+
     def sub_at(index):
         return pl.ds(pl.multiple_of(index * SUB, SUB), SUB)
 
@@ -133,7 +139,7 @@
 
     def row_copy(i, side):
         device = (sec, targets[i] * nz + mz)
-        src, dst = rows.at[sub_at(targets[i]), sides[side]], ag.at[0, 0, sub(i), sides[side]]
+        src, dst = rows.at[sub_at(targets[i]), quarters[side]], ag.at[0, 0, sub(i), quarters[side]]
         return remote(src, dst, xs_send.at[i - 1, side], xs_recv.at[i - 1, side], device)
 
     def gate_copy(i):
@@ -144,19 +150,19 @@
 
     def own_copy(d, i, cols):
         src, dst = ag.at[0, 0, sub(i), cols], ag.at[1, d, sub(i), cols]
-        return remote(src, dst, ag_send.at[d], ag_recv.at[1, d, i], out_way[d])
-
-    def out_copy(s, d, i):
-        src, dst = ag.at[s, d, sub(i)], ag.at[s + 1, d, sub(i)]
-        return remote(src, dst, ag_send.at[s + 1], ag_recv.at[s + 1, d, i], out_way[d])
-
-    def far_copy(d, i):
-        src, dst = ag.at[half - 1, d, sub(i), sides[d]], ag.at[0, 1, sub(i), sides[d]]
-        return remote(src, dst, ag_send.at[half + d], ag_recv.at[0, d, i], out_way[d])
+        return remote(src, dst, ag_send.at[d], ag_recv.at[1, d, i // 2], out_way[d])
+
+    def out_copy(s, d, p):
+        src, dst = ag.at[s, d, pair(p)], ag.at[s + 1, d, pair(p)]
+        return remote(src, dst, ag_send.at[s + 1], ag_recv.at[s + 1, d, p], out_way[d])
+
+    def far_copy(d, p):
+        src, dst = ag.at[half - 1, d, pair(p), sides[d]], ag.at[0, 1, pair(p), sides[d]]
+        return remote(src, dst, ag_send.at[half + d], ag_recv.at[0, d, p], out_way[d])
 
     for d in range(2):
         own_copy(d, 0, pl.ds(0, width)).start()
-    pieces = [(i, side) for group in (seq[1:3], seq[3:]) for side in range(2) for i in group]
+    pieces = [(i, side) for part_of in (seq[1:3], seq[3:]) for side in range(4) for i in part_of]
     for i, side in pieces:
         row_copy(i, side).start()
     for i in range(1, nx):
@@ -168,13 +174,10 @@
         for h in range(2)
         for k, (src, dst) in enumerate(((xin, near), (plr, near_plr)))
     ]
-    near_copies[0].start()
-    near_copies[2].start()
-
     for i, side in pieces:
         row_copy(i, side).wait_recv()
         for d in range(2):
-            own_copy(d, i, sides[side]).start()
+            own_copy(d, i, quarters[side]).start()
 
     for load in loads[6:]:
         load.wait()
@@ -191,6 +194,8 @@
         sig = jax.nn.sigmoid(value)
         saved[column] = sig * (1.0 + value * (1.0 - sig))
 
+    near_copies[0].start()
+    near_copies[2].start()
     for h in range(2):
         pairs = [[places[h][e], blank] for e in range(nx)] + [[blank, places[h][e]] for e in range(nx)]
         spots = jnp.concatenate([piece for pair in pairs for piece in pair])
@@ -242,16 +247,16 @@
 
     @pl.loop(1, half - 1)
     def _(s):
-        for i in seq:
+        for p in twos:
             for d in range(2):
-                out_copy(s - 1, d, i).wait_recv()
-                out_copy(s, d, i).start()
+                out_copy(s - 1, d, p).wait_recv()
+                out_copy(s, d, p).start()
         compute(s, 0, both(s))
 
-    for i in seq:
-        for d in range(2):
-            out_copy(half - 2, d, i).wait_recv()
-            far_copy(d, i).start()
+    for p in twos:
+        for d in range(2):
+            out_copy(half - 2, d, p).wait_recv()
+            far_copy(d, p).start()
     compute(half - 1, 0, both(half - 1))
 
     def level_copy(k, to, d):
@@ -279,13 +284,13 @@
     def term(s, d, i, side):
         return part[s, d, sub(i), sides[side]].astype(f32)
 
-    def back_copy(s, d, i):
-        src, dst = rs.at[s, d, sub(i)], rs.at[s - 1, d, sub(i)]
-        return remote(src, dst, rs_send.at[s], rs_recv.at[s - 1, d, i], back_way[d])
+    def back_copy(s, d, p):
+        src, dst = rs.at[s, d, pair(p)], rs.at[s - 1, d, pair(p)]
+        return remote(src, dst, rs_send.at[s], rs_recv.at[s - 1, d, p], back_way[d])
 
     def half_copy(d, i, side):
         src, dst = rs.at[half - 1, d, sub(i), sides[side]], rs.at[half - 2, d, sub(i), sides[side]]
-        return remote(src, dst, rs_send.at[half - 1], rs_recv.at[half - 2, d, i], back_way[d])
+        return remote(src, dst, rs_send.at[half - 1], rs_recv.at[half - 2, d, i // 2], back_way[d])
 
     def first_copy(d, i):
         src, dst = stage.at[sub(i), sides[d]], rs.at[half - 1, d, sub(i), sides[d]]
@@ -301,9 +306,9 @@
         for d in range(2):
             write(rs.at[half - 1, d], i, 1 - d, term(half - 1, d, i, 1 - d), half, d)
             half_copy(d, i, 1 - d).start()
-    for i in seq:
-        for d in range(2):
-            far_copy(d, i).wait_recv()
+    for p in twos:
+        for d in range(2):
+            far_copy(d, p).wait_recv()
     compute(0, 1, (lax.rem(mz + half, nz),))
     for d in range(2):
         send_level(0, half - 1, d, bound[0, 1])
@@ -330,14 +335,15 @@
         level_copy(half - 1, half - 2, d).wait_recv()
         most = jnp.maximum(bound_in(half, d), bound_in(half - 2, d))
         send_level(half - 2, half - 3, d, most + bound[half - 2, d])
-    for i in back_seq:
-        for d in range(2):
-            back_copy(half - 1, d, i).wait_recv()
+    for p in twos[::-1]:
+        for d in range(2):
+            back_copy(half - 1, d, p).wait_recv()
             ref = rs.at[half - 2, d]
-            for side in range(2):
-                level = half - 2 if side == d else half
-                write(ref, i, side, read(ref, i, side, level, d) + term(half - 2, d, i, side), half - 2, d)
-            back_copy(half - 2, d, i).start()
+            for i in (2 * p, 2 * p + 1):
+                for side in range(2):
+                    level = half - 2 if side == d else half
+                    write(ref, i, side, read(ref, i, side, level, d) + term(half - 2, d, i, side), half - 2, d)
+            back_copy(half - 2, d, p).start()
     settle(half - 2)
 
     @pl.loop(1, half - 3)
@@ -346,21 +352,23 @@
         for d in range(2):
             level_copy(s + 1, s, d).wait_recv()
             send_level(s, s - 1, d, bound_in(s, d) + bound[s, d])
-        for i in back_seq:
+        for p in twos[::-1]:
             for d in range(2):
-                back_copy(s + 1, d, i).wait_recv()
+                back_copy(s + 1, d, p).wait_recv()
                 ref = rs.at[s, d]
-                for side in range(2):
-                    write(ref, i, side, read(ref, i, side, s, d) + term(s, d, i, side), s, d)
-                back_copy(s, d, i).start()
+                for i in (2 * p, 2 * p + 1):
+                    for side in range(2):
+                        write(ref, i, side, read(ref, i, side, s, d) + term(s, d, i, side), s, d)
+                back_copy(s, d, p).start()
         settle(s)
 
     for d in range(2):
         level_copy(2, 1, d).wait_recv()
         send_level(1, 0, d, bound_in(1, d) + bound[1, d])
-    for i in back_seq:
-        for d in range(2):
-            back_copy(2, d, i).wait_recv()
+    for k, i in enumerate(back_seq):
+        for d in range(2):
+            if k % 2 == 0:
+                back_copy(2, d, i // 2).wait_recv()
         for side in range(2):
             for d in range(2):
                 ref = rs.at[1, d]
@@ -371,8 +379,6 @@
     for i in range(1, nx):
         gate_copy(i).wait_recv()
 
-    quarter = fold // 2
-
     def y_copy(h, i, side):
         device = ((sec_up, sec_down)[h], columns[i] * nz + mz)
         cols = pl.ds(side * quarter, quarter)
@@ -380,7 +386,7 @@
         return remote(src, dst, y_send.at[h], y_recv.at[h, mx], device)
 
     for i in range(1, nx):
-        for side in range(2):
+        for side in range(4):
             row_copy(i, side).wait_send()
         gate_copy(i).wait_send()
     for d in range(2):
@@ -487,7 +493,7 @@
             pltpu.VMEM((2, tokens, 2 * span), bf16),
             pltpu.VMEM((2, span, width // 2), bf16),
             dma((9,)),
-            dma((nx - 1, 2)), dma((nx - 1, 2)), dma((nx - 1,)), dma((nx - 1,)),
+            dma((nx - 1, 4)), dma((nx - 1, 4)), dma((nx - 1,)), dma((nx - 1,)),
             dma((half + 2,)), dma((half, 2, nx)),
             dma((half,)), dma((half, 2, nx)),
             dma((2, 2)), dma((2, 2)), dma((2,)), dma((2, nx)), dma((2, nx, 2)), dma((half + 1, 2)), dma((half + 1, 2)),

time: 173 us -> 174 us (level)
  no operation moved by 1% of the time
where the time goes in v7:
time: 174 us; the launch traced here: 173 us
  Pallas kernels  173 us (99%)
    pallas_call x1, Pallas kernels, per_device(): pl.pallas_call(functools.partial(kernel, nsec, nx, nz), out_shape=[pltpu....  171 us

profile of v7, /device:TPU:1, one launch (start us, length us, event | category | flops | bytes accessed | tf_op | source)
XLA Modules:
  0.0 173.4 jit_solution(17695615309567107492)
XLA Ops:
  0.6 171.4 %shard_map.104 = (bf16[2,96,3584]{2,1,0:T(8,128)(2,1)S(1)}, bf16[2,96,128]{2,1,0:T(8,128)(2,1)S(1)}, bf16[2,64,1792]{2,1,0:T(8,128)(2,1)S(1)}) custom-call(bf16[96,3584]{1,0:T(8,128)(2,1)} %bitcast.21, bf16[96,3584]{1,0:T(8,128)(2,1)} %bitcast.22, s32[8,96]{1,0:T(8,128)} %bitcast.24, f32[8,96]{1,0:T(8,128)} %bitcast.25, s32[8,96]{1,0:T(8,128)} %bitcast.26, ...), custom_call_target="tpu_custom_call" | custom-call | tf_op jit(solution)/shard_map/pallas_call | solution.py:467
  172.1 1.4 shard_map.105

commit v8 on v6

--- a/solution.py
+++ b/solution.py
@@ -67,6 +67,8 @@
     seq = (0, 1, 3, 2) if nx == 4 else tuple(range(nx))
     back_seq = seq[::-1]
     sides = (pl.ds(0, fold), pl.ds(fold, fold))
+    quarter = fold // 2
+    quarters = [pl.ds(k * quarter, quarter) for k in range(4)]
     group = 128 // nx
 
     sec = lax.axis_index("section")
@@ -133,7 +135,7 @@
 
     def row_copy(i, side):
         device = (sec, targets[i] * nz + mz)
-        src, dst = rows.at[sub_at(targets[i]), sides[side]], ag.at[0, 0, sub(i), sides[side]]
+        src, dst = rows.at[sub_at(targets[i]), quarters[side]], ag.at[0, 0, sub(i), quarters[side]]
         return remote(src, dst, xs_send.at[i - 1, side], xs_recv.at[i - 1, side], device)
 
     def gate_copy(i):
@@ -156,7 +158,7 @@
 
     for d in range(2):
         own_copy(d, 0, pl.ds(0, width)).start()
-    pieces = [(i, side) for group in (seq[1:3], seq[3:]) for side in range(2) for i in group]
+    pieces = [(i, side) for part_of in (seq[1:3], seq[3:]) for side in range(4) for i in part_of]
     for i, side in pieces:
         row_copy(i, side).start()
     for i in range(1, nx):
@@ -168,13 +170,10 @@
         for h in range(2)
         for k, (src, dst) in enumerate(((xin, near), (plr, near_plr)))
     ]
-    near_copies[0].start()
-    near_copies[2].start()
-
     for i, side in pieces:
         row_copy(i, side).wait_recv()
         for d in range(2):
-            own_copy(d, i, sides[side]).start()
+            own_copy(d, i, quarters[side]).start()
 
     for load in loads[6:]:
         load.wait()
@@ -191,6 +190,8 @@
         sig = jax.nn.sigmoid(value)
         saved[column] = sig * (1.0 + value * (1.0 - sig))
 
+    near_copies[0].start()
+    near_copies[2].start()
     for h in range(2):
         pairs = [[places[h][e], blank] for e in range(nx)] + [[blank, places[h][e]] for e in range(nx)]
         spots = jnp.concatenate([piece for pair in pairs for piece in pair])
@@ -371,8 +372,6 @@
     for i in range(1, nx):
         gate_copy(i).wait_recv()
 
-    quarter = fold // 2
-
     def y_copy(h, i, side):
         device = ((sec_up, sec_down)[h], columns[i] * nz + mz)
         cols = pl.ds(side * quarter, quarter)
@@ -380,7 +379,7 @@
         return remote(src, dst, y_send.at[h], y_recv.at[h, mx], device)
 
     for i in range(1, nx):
-        for side in range(2):
+        for side in range(4):
             row_copy(i, side).wait_send()
         gate_copy(i).wait_send()
     for d in range(2):
@@ -437,10 +436,9 @@
                 spots = place[:, k * span : (k + 1) * span]
                 here = jnp.dot(spots, share, preferred_element_type=f32)
                 done[h, :, cols] = jnp.where(with_share, here, near[h, :, cols].astype(f32)).astype(bf16)
-            cols = pl.ds(side * fold, fold)
-            store = pltpu.make_async_copy(done.at[h, :, cols], (outf, outb)[h].at[:, cols], out_sem.at[h, side])
-            store.start()
-            stores.append(store)
+                store = pltpu.make_async_copy(done.at[h, :, cols], (outf, outb)[h].at[:, cols], out_sem.at[h, 2 * side + k])
+                store.start()
+                stores.append(store)
     for store in stores:
         store.wait()
 
@@ -487,7 +485,7 @@
             pltpu.VMEM((2, tokens, 2 * span), bf16),
             pltpu.VMEM((2, span, width // 2), bf16),
             dma((9,)),
-            dma((nx - 1, 2)), dma((nx - 1, 2)), dma((nx - 1,)), dma((nx - 1,)),
+            dma((nx - 1, 4)), dma((nx - 1, 4)), dma((nx - 1,)), dma((nx - 1,)),
             dma((half + 2,)), dma((half, 2, nx)),
             dma((half,)), dma((half, 2, nx)),
             dma((2, 2)), dma((2, 2)), dma((2,)), dma((2, nx)), dma((2, nx, 2)), dma((half + 1, 2)), dma((half + 1, 2)),
@@ -504,7 +502,7 @@
         out_shape=[jax.ShapeDtypeStruct((tokens, width), bf16)] * 2,
         in_specs=[vmem] * 3,
         out_specs=[any_space] * 2,
-        scratch_shapes=[pltpu.VMEM((2, tokens, width), bf16), dma((2, 2))],
+        scratch_shapes=[pltpu.VMEM((2, tokens, width), bf16), dma((2, 4))],
         compiler_params=pltpu.CompilerParams(vmem_limit_bytes=32 * 1024 * 1024),
     )(*(pltpu.with_memory_space_constraint(v, pltpu.VMEM) for v in (near, near_plr, yrecv)))
     return (outs[0][None], outs[1][None])

time: 173 us -> 172 us (level)
  no operation moved by 1% of the time
where the time goes in v8:
time: 172 us
  Pallas kernels  171 us (99%)
    pallas_call x1, Pallas kernels, per_device(): pl.pallas_call(functools.partial(kernel, nsec, nx, nz), out_shape=[pltpu....  170 us

profile of v8, /device:TPU:1, one launch (start us, length us, event | category | flops | bytes accessed | tf_op | source)
XLA Modules:
  0.0 172.1 jit_solution(16549948734224535501)
XLA Ops:
  0.6 170.2 %shard_map.104 = (bf16[2,96,3584]{2,1,0:T(8,128)(2,1)S(1)}, bf16[2,96,128]{2,1,0:T(8,128)(2,1)S(1)}, bf16[2,64,1792]{2,1,0:T(8,128)(2,1)S(1)}) custom-call(bf16[96,3584]{1,0:T(8,128)(2,1)} %bitcast.21, bf16[96,3584]{1,0:T(8,128)(2,1)} %bitcast.22, s32[8,96]{1,0:T(8,128)} %bitcast.24, f32[8,96]{1,0:T(8,128)} %bitcast.25, s32[8,96]{1,0:T(8,128)} %bitcast.26, ...), custom_call_target="tpu_custom_call" | custom-call | tf_op jit(solution)/shard_map/pallas_call | solution.py:459
  170.8 1.3 shard_map.105
